TPU v7x, 256 devices: a whole 4x4x8 slice. The times are simulated.
256 devices in a mesh: seq: 32 (over y, x, core), kvh: 8 (over z).
Axes of the slice: x: 4, y: 4, z: 8, core: 2. Of those that a mesh axis runs over, the one named last changes fastest.
Arguments:
- query: bfloat16 [4, 128, 128], P(None, 'kvh'), may hold values from -4 to 4
- key_cache: bfloat16 [4, 16384, 8, 128], P(None, 'seq', 'kvh'), may hold values from -5.5 to 5.5
- value_cache: bfloat16 [4, 16384, 8, 128], P(None, 'seq', 'kvh'), may hold values from -5 to 5
- lengths: int32 [4], replicated, may hold values from 8192 to 16384, as said below
- residual: float32 [4, 16384], P(None, ('seq', 'kvh')), may hold values from -32 to 32
- out_weight: bfloat16 [8, 2048, 16384], P('kvh', 'seq'), may hold values from -0.09375 to 0.09375
- norm_gain: float32 [16384], P('seq'), may hold values from 0.25 to 1.75
- gate_weight: bfloat16 [16384, 26624], P('seq', 'kvh'), may hold values from -0.046875 to 0.046875
- up_weight: bfloat16 [16384, 26624], P('seq', 'kvh'), may hold values from -0.046875 to 0.046875
- down_weight: bfloat16 [26624, 16384], P('kvh', 'seq'), may hold values from -0.0625 to 0.0625
Outputs:
- next_hidden: float32 [4, 16384], P(None, ('seq', 'kvh'))
Inputs may be any that keep to these rules, and one draw needn't show every extreme that they name: `lengths`: each a multiple of 128; one request has exactly 16384 and one exactly 8192.
All inputs are finite; a program needn't handle non-finite values.
Results may differ from a plain program's by a relative error of at most 0.0017.
Values may be sent and summed in bfloat16 or wider, within the bound.
No kernel may reach another device: no remote copies, remote signals or barrier semaphores. Data moves between devices by JAX's collectives and lax.ppermute only.
A program may use at most 64 MiB of HBM per device.

v0:
```python
import jax
import jax.numpy as jnp
from jax import lax
from jax.sharding import PartitionSpec as P

D = 16384


EPSILON = 1e-05
MASKED = -1e30


def on_device(
    query,
    key_cache,
    value_cache,
    lengths,
    residual,
    out_weight,
    norm_gain,
    gate_weight,
    up_weight,
    down_weight,
):
    seq_count = lax.axis_size("seq")
    seq_index = lax.axis_index("seq")
    kvh_index = lax.axis_index("kvh")
    batch = key_cache.shape[0]
    positions_here = key_cache.shape[1]
    head_dim = key_cache.shape[3]
    heads = query.shape[1]
    keys = key_cache[:, :, 0, :]
    values = value_cache[:, :, 0, :]
    scores = jnp.einsum(
        "bhd,bpd->bhp", query, keys, preferred_element_type=jnp.float32
    ) * head_dim ** (-0.5)
    positions = seq_index * positions_here + lax.broadcasted_iota(
        jnp.int32, (1, 1, positions_here), 2
    )
    live = positions < lengths[:, None, None]
    masked = jnp.where(live, scores, MASKED)
    local_max = jnp.max(masked, axis=2)
    weights = jnp.where(live, jnp.exp(masked - local_max[:, :, None]), 0.0)
    local_sum = jnp.sum(weights, axis=2)
    partial_out = jnp.einsum(
        "bhp,bpd->bhd", weights, values.astype(jnp.float32), precision=lax.Precision.HIGHEST
    )
    piece = heads * head_dim // seq_count
    per_piece = max(1, piece // head_dim)
    repeats = seq_count * per_piece // heads
    flat_out = partial_out.reshape(batch, seq_count, piece)
    max_pieces = jnp.repeat(local_max, repeats, axis=1).reshape(batch, seq_count, per_piece)
    sum_pieces = jnp.repeat(local_sum, repeats, axis=1).reshape(batch, seq_count, per_piece)
    got_out, got_max, got_sum = (
        lax.all_to_all(flat_out, "seq", split_axis=1, concat_axis=1, tiled=True),
        lax.all_to_all(max_pieces, "seq", split_axis=1, concat_axis=1, tiled=True),
        lax.all_to_all(sum_pieces, "seq", split_axis=1, concat_axis=1, tiled=True),
    )
    top = jnp.max(got_max, axis=1, keepdims=True)
    factor = jnp.exp(got_max - top)
    total = jnp.sum(factor * got_sum, axis=1)
    width_sub = piece // per_piece
    merged = jnp.sum(
        got_out.reshape(batch, seq_count, per_piece, width_sub) * factor[:, :, :, None], axis=1
    )
    attention = (merged / total[:, :, None]).reshape(batch, piece).astype(jnp.bfloat16)
    projected = jnp.dot(attention, out_weight[0], preferred_element_type=jnp.float32)
    columns = residual.shape[1]
    carried = (
        lax.psum_scatter(projected, ("seq", "kvh"), scatter_dimension=1, tiled=True) + residual
    )
    squares = lax.psum(jnp.sum(carried * carried, axis=1), ("seq", "kvh"))
    scale_rows = lax.rsqrt(squares / D + EPSILON)
    gain_cols = lax.dynamic_slice_in_dim(norm_gain, kvh_index * columns, columns, 0)
    normed_cols = (carried * scale_rows[:, None] * gain_cols[None, :]).astype(jnp.bfloat16)
    normed = lax.all_gather(normed_cols, "kvh", axis=1, tiled=True)
    gate_term = jnp.dot(normed, gate_weight, preferred_element_type=jnp.float32)
    up_term = jnp.dot(normed, up_weight, preferred_element_type=jnp.float32)
    gate_full, up_full = lax.psum((gate_term, up_term), "seq")
    activated = (jax.nn.silu(gate_full) * up_full).astype(jnp.bfloat16)
    down_term = jnp.dot(activated, down_weight, preferred_element_type=jnp.float32)
    ffn_cols = lax.psum_scatter(down_term, "kvh", scatter_dimension=1, tiled=True)
    return carried + ffn_cols


def solution(mesh):
    return jax.shard_map(
        on_device,
        mesh=mesh,
        in_specs=(
            P(None, "kvh", None),
            P(None, "seq", "kvh", None),
            P(None, "seq", "kvh", None),
            P(),
            P(None, ("seq", "kvh")),
            P("kvh", "seq", None),
            P("seq"),
            P("seq", "kvh"),
            P("seq", "kvh"),
            P("kvh", "seq"),
        ),
        out_specs=P(None, ("seq", "kvh")),
        check_vma=False,
    )
```

profile of v0, /device:TPU:1, one launch (start us, length us, event | category | flops | bytes accessed | tf_op | source)
XLA Modules:
  0.0 1576.6 jit_solution(589657193804364845)
XLA Ops:
  6.5 0.0 copy-start
  6.5 0.9 broadcast_compare_fusion
  7.4 0.0 copy-start.3
  7.4 0.6 copy-done.3
  8.0 1.4 fusion.20
  9.4 0.0 copy-start.2
  9.4 0.1 copy.25
  9.5 0.6 broadcast_in_dim.34
  10.1 0.0 copy-done.2
  10.1 8.6 all-to-all-start.1
  18.7 1.4 fusion.5
  20.1 1.3 copy.29
  21.4 4.2 all-to-all-done.1
  25.6 1.3 broadcast_in_dim.35
  26.9 4.7 all-to-all-start.2
  31.6 2.1 fusion.2
  33.7 0.8 reshape.96
  34.6 0.7 reshape.103
  35.3 0.1 copy.27
  35.4 0.1 reduce_max.19
  35.4 3.3 all-to-all-done.2
  38.8 4.2 all-to-all-start
  42.9 0.0 reduce-scatter.7.cloned.1.call-start
  43.0 0.8 copy.31
  43.8 0.2 multiply_reduce_fusion.2
  44.0 0.1 copy.28
  44.0 6.1 all-to-all-done
  50.2 0.5 broadcast.61
  50.7 0.7 reduce.4
  51.4 0.1 reshape.104
  51.5 0.1 multiply_reduce_fusion
  51.6 6.6 convolution_bitcast_fusion
  58.2 0.0 copy-start.4
  58.2 0.0 reduce-scatter.7.cloned.1.call-update
  58.2 0.0 all-reduce.3.cloned.1.call-start
  58.3 0.8 dynamic_slice.3
  59.0 1262.7 %reduce-scatter.7.cloned.1.call-done = f32[64,4]{1,0:T(8,128)} async-done(((f32[16384,4]{1,0:T(8,128)}), f32[64,4]{1,0:T(8,128)}) %reduce-scatter.7.cloned.1.call-update) | async-done | bytes 1040
  1321.8 0.8 copy.34
  1322.6 0.0 copy-done.4
  1322.6 0.1 multiply_reduce_fusion.1
  1322.7 88.6 %psum.21 = f32[4]{0:T(128)S(1)} all-reduce(f32[4]{0:T(128)S(1)} %get-tuple-element.7), channel_id=1, replica_groups=mesh['seq'=32,'kvh'=8] {'seq','kvh'}, use_global_device_ids=true, to_apply=%region_7.8 | all-reduce | flops 4 | bytes 32 | tf_op jit(solution)/shard_map/psum | solution.py:72
  1411.3 0.1 fusion.15
  1411.4 11.2 all-gather
  1422.6 0.1 reshape.98
  1422.7 0.0 copy-done
  1422.7 0.0 copy-start.1
  1422.7 1.2 fusion.21
  1423.8 0.8 copy-done.1
  1424.6 1.2 fusion.22
  1425.8 0.0 all-reduce.3.cloned.1.call-update
  1425.8 0.0 reduce-scatter.9.cloned.1.call-start
  1425.9 108.6 %all-reduce.3.cloned.1.call-done = (f32[4,3328]{1,0:T(4,128)}, f32[4,3328]{1,0:T(4,128)}) async-done(((f32[4,3328]{1,0:T(4,128)}, f32[4,3328]{1,0:T(4,128)}), (f32[4,3328]{1,0:T(4,128)}, f32[4,3328]{1,0:T(4,128)})) %all-reduce.3.cloned.1.call-update) | async-done | bytes 106512 | tf_op jit(solution)/shard_map/psum | solution.py:79
  1534.5 4.2 convolution_bitcast_fusion.1
  1538.6 0.0 reduce-scatter.9.cloned.1.call-update
  1538.7 30.0 %reduce-scatter.9.cloned.1.call-done = f32[64,4]{1,0:T(8,128)} async-done(((f32[512,4]{1,0:T(8,128)}), f32[64,4]{1,0:T(8,128)}) %reduce-scatter.9.cloned.1.call-update) | async-done | bytes 1040
  1568.6 0.8 copy.36
  1569.5 0.6 add.43
  (4 shorter events, 0.1 us)
Async XLA Ops:
  6.5 1416.1 %copy-start = (bf16[512,3328]{1,0:T(8,128)(2,1)S(1)}, bf16[512,3328]{1,0:T(8,128)(2,1)}, u32[]{:S(2)}) copy-start(bf16[512,3328]{1,0:T(8,128)(2,1)} %param.17) | copy-start | bytes 10223620
  7.4 0.6 copy-start.3
  9.4 0.7 copy-start.2
  10.1 15.5 all-to-all-start.1
  26.9 11.8 all-to-all-start.2
  38.8 11.4 all-to-all-start
  42.9 1278.8 %reduce-scatter.7.cloned.1.call-start = ((), (), s32[]{:S(2)}) async-start(), calls=%async_computation.5 | async-start | bytes 8421376
  58.2 1264.4 %copy-start.4 = (f32[4,64]{1,0:T(4,128)S(1)}, f32[4,64]{1,0:T(4,128)}, u32[]{:S(2)}) copy-start(f32[4,64]{1,0:T(4,128)} %param.14) | copy-start | bytes 3076
  58.2 1476.3 %all-reduce.3.cloned.1.call-start = ((), (), s32[]{:S(2)}) async-start(), calls=%async_computation.7 | async-start | bytes 212992 | tf_op jit(solution)/shard_map/psum | solution.py:79
  1422.7 2.0 copy-start.1
  1425.8 142.8 %reduce-scatter.9.cloned.1.call-start = ((), (), s32[]{:S(2)}) async-start(), calls=%async_computation.6 | async-start | bytes 294912
Sparse Core Ops, SparseCore 0:
  58.3 1263.3 reduce-scatter.6
  1426.0 108.4 all-reduce.2
  1538.8 29.8 reduce-scatter.8
where the time goes:
time: 1580 us
  waiting for transfers between devices  1420 us (90%)
  blocking collectives  99.8 us (6%)
  starting transfers between devices  17.6 us (1%)
  matrix products  16.5 us (1%)
    unnamed x5, waiting for transfers between devices  1290 us
    psum x1, waiting for transfers between devices, on_device(): gate_full, up_full = lax.psum((gate_term, up_term), 'seq')  109 us
    psum x1, blocking collectives, on_device(): squares = lax.psum(jnp.sum(carried * carried, axis=1), ('seq', 'kvh'))  88.6 us
  transfers between devices with their start and end apart: 6, of which 6 were waited for; matrix products, arithmetic and copies ran while one was open for 1% of the time, Pallas kernels for 0%

commit v1 on v0

v1 whole, which is shorter than its diff:
```python
import jax
import jax.numpy as jnp
from jax import lax
from jax.experimental import pallas as pl
from jax.experimental.pallas import tpu as pltpu
from jax.sharding import PartitionSpec as P

EPSILON = 1e-05
MASKED = -1e30
LANES = 128
F32 = jnp.float32
BF16 = jnp.bfloat16


def dot(a, b):
    return jnp.dot(a, b, preferred_element_type=F32)


def attend_kernel(lengths, query, keys, values, out):
    batch, heads, head_dim = query.shape
    positions_here = keys.shape[1]
    pieces = out.shape[0]
    per_head = pieces // heads
    width = head_dim // per_head
    stat = (LANES - width) // 2
    first = lax.axis_index("seq") * positions_here
    positions = first + lax.broadcasted_iota(jnp.int32, (heads, positions_here), 1)
    for b in range(batch):
        scores = lax.dot_general(
            query[b], keys[b], (((1,), (1,)), ((), ())), preferred_element_type=F32
        ) * head_dim ** (-0.5)
        live = positions < lengths[b]
        masked = jnp.where(live, scores, MASKED)
        top = jnp.max(masked, axis=1, keepdims=True)
        weights = jnp.where(live, jnp.exp(masked - top), 0.0)
        total = jnp.sum(weights, axis=1, keepdims=True)
        high = weights.astype(BF16)
        low = (weights - high.astype(F32)).astype(BF16)
        both = dot(jnp.concatenate([high, low], axis=0), values[b])
        sums = both[:heads] + both[heads:]
        stats = jnp.concatenate(
            [jnp.broadcast_to(top, (heads, stat)), jnp.broadcast_to(total, (heads, stat))], axis=1
        )
        for part in range(per_head):
            packed = jnp.concatenate([sums[:, part * width : (part + 1) * width], stats], axis=1)
            for h in range(heads):
                out[h * per_head + part, b : b + 1, :] = packed[h : h + 1]


def project_kernel(parts, weight, out):
    width = weight.shape[0]
    stat = (LANES - width) // 2
    got = parts[...]
    top = jnp.max(got[:, :, width : width + 1], axis=0)
    factor = jnp.exp(got[:, :, width : width + 1] - top[None])
    total = jnp.sum(factor * got[:, :, width + stat : width + stat + 1], axis=0)
    merged = jnp.sum(factor * got[:, :, :width], axis=0)
    attention = (merged / total).astype(BF16)
    columns = out.shape[2]
    for piece in range(out.shape[0]):
        out[piece] = dot(attention, weight[:, piece * columns : (piece + 1) * columns])


def column_mask(shape, width):
    group = lax.axis_index("kvh")
    lanes = lax.broadcasted_iota(jnp.int32, shape, len(shape) - 1)
    return (lanes >= group * width) & (lanes < (group + 1) * width)


def carry_kernel(parts, residual, out):
    summed = jnp.sum(parts[...], axis=0)
    spread = jnp.concatenate([residual[...]] * (summed.shape[1] // residual.shape[1]), axis=1)
    summed = summed + jnp.where(column_mask(summed.shape, residual.shape[1]), spread, 0.0)
    for piece in range(out.shape[0]):
        out[piece] = summed


def gate_kernel(parts, gain, gate_weight, up_weight, out, carried_out):
    batch = parts.shape[1]
    carried = jnp.sum(parts[...], axis=0)
    width = carried_out.shape[1]
    own = jnp.where(column_mask(carried.shape, width), carried, 0.0)
    carried_out[...] = sum(
        own[:, piece * width : (piece + 1) * width] for piece in range(carried.shape[1] // width)
    )
    squares = jnp.broadcast_to(
        jnp.sum(carried * carried, axis=1, keepdims=True), (batch, LANES)
    )
    scaled = (carried * gain[...]).astype(BF16)
    zeros = jnp.zeros((batch, LANES), F32)
    tiles = gate_weight.shape[1] // LANES
    for tile in range(out.shape[0]):
        if tile < tiles:
            lanes = slice(tile * LANES, (tile + 1) * LANES)
            gate = dot(scaled, gate_weight[:, lanes])
            up = dot(scaled, up_weight[:, lanes])
        else:
            gate = up = zeros
        out[tile] = jnp.concatenate([gate, up, squares, zeros], axis=0)


def activate_kernel(width, parts, out):
    batch = out.shape[1]
    summed = jnp.sum(parts[...], axis=0)
    scale = lax.rsqrt(summed[2 * batch : 3 * batch] / width + EPSILON)
    gate = summed[:batch] * scale
    up = summed[batch : 2 * batch] * scale
    activated = (gate / (1.0 + jnp.exp(-gate)) * up).astype(BF16).astype(F32)
    for piece in range(out.shape[0]):
        out[piece] = activated


def down_kernel(activated, weight, out):
    tiles = weight.shape[0] // LANES
    full = jnp.concatenate([activated[tile] for tile in range(tiles)], axis=1).astype(BF16)
    down = dot(full, weight[...])
    pieces = out.shape[0]
    width = down.shape[1] // pieces
    per_tile = LANES // width
    for piece in range(pieces):
        tile = down[:, piece // per_tile * LANES : (piece // per_tile + 1) * LANES]
        shift = piece % per_tile * width
        out[piece] = tile if shift == 0 else pltpu.roll(tile, LANES - shift, 1)


def finish_kernel(parts, carried, out):
    out[...] = carried[...] + jnp.sum(parts[...], axis=0)[:, : out.shape[1]]


VMEM = pl.BlockSpec(memory_space=pltpu.VMEM)
SMEM = pl.BlockSpec(memory_space=pltpu.SMEM)


def call(kernel, shapes, specs, *args):
    return pl.pallas_call(
        kernel,
        out_shape=shapes,
        in_specs=specs,
        out_specs=jax.tree.map(lambda _: VMEM, shapes),
        compiler_params=pltpu.CompilerParams(vmem_limit_bytes=24 * 1024 * 1024),
    )(*args)


def swap(array, axis):
    return lax.all_to_all(array, axis, split_axis=0, concat_axis=0, tiled=True)


def on_device(
    query,
    key_cache,
    value_cache,
    lengths,
    residual,
    out_weight,
    norm_gain,
    gate_weight,
    up_weight,
    down_weight,
):
    seq_count = lax.axis_size("seq")
    kvh_count = lax.axis_size("kvh")
    batch = query.shape[0]
    columns = norm_gain.shape[0]
    own = residual.shape[1]

    def shape(*dims):
        return jax.ShapeDtypeStruct(dims, F32)

    with jax.named_scope("attend"):
        partial = call(
            attend_kernel,
            shape(seq_count, batch, LANES),
            [SMEM, VMEM, VMEM, VMEM],
            lengths,
            query,
            key_cache[:, :, 0, :],
            value_cache[:, :, 0, :],
        )
    partial = swap(partial, "seq")
    with jax.named_scope("project"):
        projected = call(
            project_kernel, shape(seq_count, batch, columns), [VMEM] * 2, partial, out_weight[0]
        )
    projected = swap(projected, "seq")
    with jax.named_scope("carry"):
        carried = call(
            carry_kernel, shape(kvh_count, batch, columns), [VMEM] * 2, projected, residual
        )
    carried = swap(carried, "kvh")
    with jax.named_scope("gate_up"):
        hidden, own_carried = call(
            gate_kernel,
            (shape(seq_count, 4 * batch, LANES), shape(batch, own)),
            [VMEM] * 4,
            carried,
            norm_gain.reshape(1, columns),
            gate_weight,
            up_weight,
        )
    hidden = swap(hidden, "seq")
    with jax.named_scope("activate"):
        width = seq_count * columns
        activated = call(
            lambda parts, out: activate_kernel(width, parts, out),
            shape(seq_count, batch, LANES),
            [VMEM],
            hidden,
        )
    activated = swap(activated, "seq")
    with jax.named_scope("down"):
        down = call(down_kernel, shape(kvh_count, batch, LANES), [VMEM] * 2, activated, down_weight)
    down = swap(down, "kvh")
    with jax.named_scope("finish"):
        return call(finish_kernel, shape(batch, own), [VMEM] * 2, down, own_carried)


def solution(mesh):
    return jax.shard_map(
        on_device,
        mesh=mesh,
        in_specs=(
            P(None, "kvh", None),
            P(None, "seq", "kvh", None),
            P(None, "seq", "kvh", None),
            P(),
            P(None, ("seq", "kvh")),
            P("kvh", "seq", None),
            P("seq"),
            P("seq", "kvh"),
            P("seq", "kvh"),
            P("kvh", "seq"),
        ),
        out_specs=P(None, ("seq", "kvh")),
        check_vma=False,
    )
```

time: 1580 us -> 90 us (0.06)
  waiting for transfers between devices: 1420 us -> 0 us
  blocking collectives: 99.8 us -> 77.1 us
  starting transfers between devices: 17.6 us -> 0 us
  matrix products: 16.5 us -> 0 us
    unnamed x5 -> x0, waiting for transfers between devices: 1290 us -> none
    psum x1 -> x0, waiting for transfers between devices: 109 us -> none  [on_device(): gate_full, up_full = lax.psum((gate_term, up_term), 'seq')]
    psum x1 -> x0, blocking collectives: 88.6 us -> none  [on_device(): squares = lax.psum(jnp.sum(carried * carried, axis=1), ('seq', 'kvh'))]
    all_to_all x0 -> x6, blocking collectives: none -> 77.1 us  [swap(): return lax.all_to_all(array, axis, split_axis=0, concat_axis=0, tiled=True)]
    all_to_all x3 -> x0, starting transfers between devices: 17.5 us -> none  [the longest x1 8.59 us: on_device(): lax.all_to_all(max_pieces, 'seq', split_axis=1, concat_axis=1, tiled=True)]
  transfers between devices with their start and end apart: 6 -> 0, of which waited for: 6 -> 0; matrix products, arithmetic and copies ran while one was open for 1% -> 0% of each run, Pallas kernels for 0% -> 0%
where the time goes in v1:
time: 90 us; the launch traced here: 89.6 us
  blocking collectives  77.1 us (86%)
  local copies, waits for them, and re-layouts  7.85 us (9%)
  Pallas kernels  4.6 us (5%)
    all_to_all x6, blocking collectives, swap(): return lax.all_to_all(array, axis, split_axis=0, concat_axis=0, tiled=True)  77.1 us
    unnamed x20, local copies, waits for them, and re-layouts  7.85 us
    pallas_call x7, Pallas kernels, call(): pl.pallas_call(kernel, out_shape=shapes, in_specs=specs, out_specs=jax.tr...  4.6 us

profile of v1, /device:TPU:1, one launch (start us, length us, event | category | flops | bytes accessed | tf_op | source)
XLA Modules:
  0.0 89.6 jit_solution(2893278640102520622)
XLA Ops:
  0.0 0.0 copy-start
  0.0 0.0 copy-start.4
  0.0 1.2 %copy-done.4 = bf16[4,512,1,128]{3,1,2,0:T(8,128)(2,1)S(1)} copy-done((bf16[4,512,1,128]{3,1,2,0:T(8,128)(2,1)S(1)}, bf16[4,512,1,128]{3,1,2,0:T(8,128)(2,1)}, u32[]{:S(2)}) %copy-start.4) | copy-done | bytes 524312
  1.2 0.0 copy-start.5
  1.2 1.0 %copy-done.5 = bf16[4,512,1,128]{3,1,2,0:T(8,128)(2,1)S(1)} copy-done((bf16[4,512,1,128]{3,1,2,0:T(8,128)(2,1)S(1)}, bf16[4,512,1,128]{3,1,2,0:T(8,128)(2,1)}, u32[]{:S(2)}) %copy-start.5) | copy-done | bytes 524312
  2.2 0.0 copy-start.6
  2.2 0.7 copy-done.6
  3.0 0.0 copy-start.9
  3.0 0.7 copy-done.9
  3.6 1.7 %attend.1 = f32[32,4,128]{2,1,0:T(4,128)S(1)} custom-call(s32[4]{0:T(128)S(1)} %copy-done.9, bf16[4,16,128]{2,1,0:T(8,128)(2,1)S(1)} %copy-done.6, bf16[4,512,128]{2,1,0:T(8,128)(2,1)S(1)} %bitcast.5, bf16[4,512,128]{2,1,0:T(8,128)(2,1)S(1)} %bitcast.6), custom_call_target="tpu_custom_call" | custom-call | tf_op jit(solution)/shard_map/attend/pallas_call | solution.py:135
  5.3 15.7 %all_to_all.30.parts = f32[32,4,128]{2,1,0:T(4,128)S(1)} all-to-all(f32[32,4,128]{2,1,0:T(4,128)S(1)} %attend.1), channel_id=1, replica_groups=mesh['seq'=32,'kvh'=8] {'seq'}, dimensions={0} | all-to-all | bytes 131072 | tf_op jit(solution)/shard_map/all_to_all | solution.py:145
  21.0 0.0 copy-start.3
  21.0 1.6 %copy-done.3 = bf16[1,64,16384]{2,1,0:T(8,128)(2,1)S(1)} copy-done((bf16[1,64,16384]{2,1,0:T(8,128)(2,1)S(1)}, bf16[1,64,16384]{2,1,0:T(8,128)(2,1)}, u32[]{:S(2)}) %copy-start.3) | copy-done | bytes 2097176
  22.6 0.0 copy-start.7
  22.6 0.5 project.1
  23.2 12.5 %all_to_all.31.parts = f32[32,4,512]{2,1,0:T(4,128)S(1)} all-to-all(f32[32,4,512]{2,1,0:T(4,128)S(1)} %project.1), channel_id=1, replica_groups=mesh['seq'=32,'kvh'=8] {'seq'}, dimensions={0} | all-to-all | bytes 524288 | tf_op jit(solution)/shard_map/all_to_all | solution.py:145
  35.6 0.0 copy-start.8
  35.6 0.7 copy-done.8
  36.3 0.1 carry.1
  36.4 15.2 %all_to_all.32.parts = f32[8,4,512]{2,1,0:T(4,128)S(1)} all-to-all(f32[8,4,512]{2,1,0:T(4,128)S(1)} %carry.1), channel_id=1, replica_groups=mesh['seq'=32,'kvh'=8] {'kvh'}, dimensions={0} | all-to-all | bytes 131072 | tf_op jit(solution)/shard_map/all_to_all | solution.py:145
  51.6 0.0 copy-done
  51.6 0.0 copy-done.7
  51.6 0.0 copy-start.1
  51.6 2.0 %copy-done.1 = bf16[512,3328]{1,0:T(8,128)(2,1)S(1)} copy-done((bf16[512,3328]{1,0:T(8,128)(2,1)S(1)}, bf16[512,3328]{1,0:T(8,128)(2,1)}, u32[]{:S(2)}) %copy-start.1) | copy-done | bytes 3407896
  53.6 0.0 copy-start.2
  53.6 1.0 %gate_up.1 = (f32[32,16,128]{2,1,0:T(8,128)S(1)}, f32[4,64]{1,0:T(4,128)S(1)}) custom-call(f32[8,4,512]{2,1,0:T(4,128)S(1)} %all_to_all.32.parts, f32[1,512]{1,0:T(1,128)S(1)} %bitcast.7, bf16[512,3328]{1,0:T(8,128)(2,1)S(1)} %copy-done, bf16[512,3328]{1,0:T(8,128)(2,1)S(1)} %copy-done.1), custom_call_target="tpu_custom_call" | custom-call | tf_op jit(solution)/shard_map/gate_up/pallas_call | solution.py:135
  54.6 13.9 %all_to_all.33.parts = f32[32,16,128]{2,1,0:T(8,128)S(1)} all-to-all(f32[32,16,128]{2,1,0:T(8,128)S(1)} %get-tuple-element.7), channel_id=1, replica_groups=mesh['seq'=32,'kvh'=8] {'seq'}, dimensions={0} | all-to-all | bytes 524288 | tf_op jit(solution)/shard_map/all_to_all | solution.py:145
  68.5 0.1 activate.1
  68.5 10.9 %all_to_all.34.activated = f32[32,4,128]{2,1,0:T(4,128)S(1)} all-to-all(f32[32,4,128]{2,1,0:T(4,128)S(1)} %activate.1), channel_id=1, replica_groups=mesh['seq'=32,'kvh'=8] {'seq'}, dimensions={0} | all-to-all | bytes 131072 | tf_op jit(solution)/shard_map/all_to_all | solution.py:145
  79.4 0.0 copy-done.2
  79.4 0.6 down.1
  80.0 9.0 %all_to_all.35.parts = f32[8,4,128]{2,1,0:T(4,128)S(1)} all-to-all(f32[8,4,128]{2,1,0:T(4,128)S(1)} %down.1), channel_id=1, replica_groups=mesh['seq'=32,'kvh'=8] {'kvh'}, dimensions={0} | all-to-all | bytes 32768 | tf_op jit(solution)/shard_map/all_to_all | solution.py:145
  89.0 0.6 finish.1
Async XLA Ops:
  0.0 51.6 %copy-start = (bf16[512,3328]{1,0:T(8,128)(2,1)S(1)}, bf16[512,3328]{1,0:T(8,128)(2,1)}, u32[]{:S(2)}) copy-start(bf16[512,3328]{1,0:T(8,128)(2,1)} %gate_weight.1) | copy-start | bytes 10223620
  0.0 1.2 %copy-start.4 = (bf16[4,512,1,128]{3,1,2,0:T(8,128)(2,1)S(1)}, bf16[4,512,1,128]{3,1,2,0:T(8,128)(2,1)}, u32[]{:S(2)}) copy-start(bf16[4,512,1,128]{3,1,2,0:T(8,128)(2,1)} %param.11) | copy-start | bytes 1572868
  1.2 1.0 %copy-start.5 = (bf16[4,512,1,128]{3,1,2,0:T(8,128)(2,1)S(1)}, bf16[4,512,1,128]{3,1,2,0:T(8,128)(2,1)}, u32[]{:S(2)}) copy-start(bf16[4,512,1,128]{3,1,2,0:T(8,128)(2,1)} %param.12) | copy-start | bytes 1572868
  2.2 0.7 copy-start.6
  3.0 0.7 copy-start.9
  21.0 1.6 %copy-start.3 = (bf16[1,64,16384]{2,1,0:T(8,128)(2,1)S(1)}, bf16[1,64,16384]{2,1,0:T(8,128)(2,1)}, u32[]{:S(2)}) copy-start(bf16[1,64,16384]{2,1,0:T(8,128)(2,1)} %param.15) | copy-start | bytes 6291460
  22.6 29.0 %copy-start.7 = (f32[512]{0:T(512)S(1)}, f32[512]{0:T(512)}, u32[]{:S(2)}) copy-start(f32[512]{0:T(512)} %param.16) | copy-start | bytes 6148
  35.6 0.7 copy-start.8
  51.6 2.0 %copy-start.1 = (bf16[512,3328]{1,0:T(8,128)(2,1)S(1)}, bf16[512,3328]{1,0:T(8,128)(2,1)}, u32[]{:S(2)}) copy-start(bf16[512,3328]{1,0:T(8,128)(2,1)} %up_weight.1) | copy-start | bytes 10223620
  53.6 25.8 %copy-start.2 = (bf16[3328,512]{1,0:T(8,128)(2,1)S(1)}, bf16[3328,512]{1,0:T(8,128)(2,1)}, u32[]{:S(2)}) copy-start(bf16[3328,512]{1,0:T(8,128)(2,1)} %weight.1) | copy-start | bytes 10223620

commit v2 on v1

v2 whole, which is shorter than its diff:
```python
import functools

import jax
import jax.numpy as jnp
from jax import lax
from jax.experimental import pallas as pl
from jax.experimental.pallas import tpu as pltpu
from jax.sharding import Mesh, PartitionSpec as P

EPSILON = 1e-05
MASKED = -1e30
LANES = 128
CORES = 2
F32 = jnp.float32
BF16 = jnp.bfloat16


def dot(a, b):
    return jnp.dot(a, b, preferred_element_type=F32)


def split(array):
    high = array.astype(BF16)
    return high, (array - high.astype(F32)).astype(BF16)


def attend_kernel(batch, *refs):
    lengths_hbm, query_hbm, keys_hbm, values_hbm = refs[:4]
    ahead = (len(refs) - 10) // 2
    out = refs[4 + ahead]
    lengths, query, keys, values, sems = refs[-5:]
    later = [
        pltpu.make_async_copy(refs[4 + i], refs[5 + ahead + i], sems.at[2 + 2 * batch + i])
        for i in range(ahead)
    ]
    heads, head_dim = query.shape[1:]
    positions_here = keys.shape[1]
    loads = [
        pltpu.make_async_copy(lengths_hbm, lengths, sems.at[0]),
        pltpu.make_async_copy(query_hbm, query, sems.at[1]),
    ]
    key_loads, value_loads = [], []
    for b in range(batch):
        key_loads.append(pltpu.make_async_copy(keys_hbm.at[b], keys.at[b], sems.at[2 + 2 * b]))
        value_loads.append(pltpu.make_async_copy(values_hbm.at[b], values.at[b], sems.at[3 + 2 * b]))
    for load in loads:
        load.start()
    for b in range(batch):
        key_loads[b].start()
        value_loads[b].start()
    for load in later:
        load.start()
    for load in loads:
        load.wait()
    pieces = out.shape[0]
    per_head = pieces // heads
    width = head_dim // per_head
    stat = (LANES - width) // 2
    shard = lax.axis_index("chip") * CORES + lax.axis_index("core")
    positions = shard * positions_here + lax.broadcasted_iota(jnp.int32, (heads, positions_here), 1)
    for b in range(batch):
        key_loads[b].wait()
        scores = lax.dot_general(
            query[b], keys[b], (((1,), (1,)), ((), ())), preferred_element_type=F32
        ) * head_dim ** (-0.5)
        live = positions < lengths[b]
        masked = jnp.where(live, scores, MASKED)
        top = jnp.max(masked, axis=1, keepdims=True)
        weights = jnp.where(live, jnp.exp(masked - top), 0.0)
        total = jnp.sum(weights, axis=1, keepdims=True)
        value_loads[b].wait()
        both = dot(jnp.concatenate(split(weights), axis=0), values[b])
        sums = both[:heads] + both[heads:]
        stats = jnp.concatenate(
            [jnp.broadcast_to(top, (heads, stat)), jnp.broadcast_to(total, (heads, stat))], axis=1
        )
        for part in range(per_head):
            packed = jnp.concatenate([sums[:, part * width : (part + 1) * width], stats], axis=1)
            for h in range(heads):
                out[h * per_head + part, b : b + 1, :] = packed[h : h + 1]
    for load in later:
        load.wait()


def project_kernel(parts, weight, out):
    width = weight.shape[0]
    stat = (LANES - width) // 2
    got = parts[...]
    top = jnp.max(got[:, :, width : width + 1], axis=0)
    factor = jnp.exp(got[:, :, width : width + 1] - top[None])
    total = jnp.sum(factor * got[:, :, width + stat : width + stat + 1], axis=0)
    merged = jnp.sum(factor * got[:, :, :width], axis=0)
    attention = (merged / total).astype(BF16)
    tiles = out.shape[1] // attention.shape[0]
    columns = tiles * LANES
    for piece in range(out.shape[0]):
        term = dot(attention, weight[:, piece * columns : (piece + 1) * columns])
        out[piece] = jnp.concatenate(
            [term[:, tile * LANES : (tile + 1) * LANES] for tile in range(tiles)], axis=0
        ).astype(BF16)


def column_mask(shape, width):
    group = lax.axis_index("kvh")
    lanes = lax.broadcasted_iota(jnp.int32, shape, len(shape) - 1)
    return (lanes >= group * width) & (lanes < (group + 1) * width)


def carry_kernel(parts, residual, out):
    batch = residual.shape[0]
    stacked = jnp.sum(parts[...].astype(F32), axis=0)
    summed = jnp.concatenate(
        [stacked[row : row + batch] for row in range(0, stacked.shape[0], batch)], axis=1
    )
    spread = jnp.concatenate([residual[...]] * (summed.shape[1] // residual.shape[1]), axis=1)
    summed = summed + jnp.where(column_mask(summed.shape, residual.shape[1]), spread, 0.0)
    for piece in range(out.shape[0]):
        out[piece] = summed


def gate_kernel(parts, gain, gate_weight, up_weight, keep, give, carried_out):
    batch = parts.shape[1]
    carried = jnp.sum(parts[...], axis=0)
    width = carried_out.shape[1]
    own = jnp.where(column_mask(carried.shape, width), carried, 0.0)
    carried_out[...] = sum(
        own[:, piece * width : (piece + 1) * width] for piece in range(carried.shape[1] // width)
    )
    squares = jnp.sum(carried * carried, axis=1, keepdims=True)
    terms = jnp.concatenate(split(carried * gain[...]), axis=0)
    half = gate_weight.shape[1] // CORES
    first = lax.axis_index("core") == 0
    halves = []
    for core in range(CORES):
        lanes = slice(core * half, (core + 1) * half)
        gate = dot(terms, gate_weight[:, lanes])
        up = dot(terms, up_weight[:, lanes])
        halves.append(jnp.concatenate([gate[:batch] + gate[batch:], up[:batch] + up[batch:]], axis=0))
    keep[:, :half] = jnp.where(first, halves[0], halves[1])
    give[:, :half] = jnp.where(first, halves[1], halves[0])
    squares = jnp.broadcast_to(jnp.concatenate([squares, squares], axis=0), (2 * batch, LANES))
    keep[:, half:] = squares
    give[:, half:] = squares


def pair_kernel(keep, got, out):
    batch = keep.shape[0] // 2
    summed = keep[...] + got[...]
    half = summed.shape[1] - LANES
    high, low = split(summed[:batch, half:])
    packed = jnp.concatenate(
        [summed[:, :half].astype(BF16), jnp.concatenate([high, low], axis=0)], axis=1
    )
    middle = packed.shape[1] // 2
    packed = jnp.concatenate([packed[:, :middle], packed[:, middle:]], axis=0)
    for piece in range(out.shape[0]):
        out[piece] = packed


def activate_kernel(model_width, parts, out):
    batch = out.shape[0]
    stacked = jnp.sum(parts[...].astype(F32), axis=0)
    rows = stacked.shape[0] // 2
    summed = jnp.concatenate([stacked[:rows], stacked[rows:]], axis=1)
    half = out.shape[1]
    squares = summed[:batch, half : half + 1] + summed[batch:, half : half + 1]
    scale = lax.rsqrt(squares / model_width + EPSILON)
    gate = summed[:batch, :half] * scale
    up = summed[batch:, :half] * scale
    out[...] = (gate / (1.0 + jnp.exp(-gate)) * up).astype(BF16).astype(F32)


def down_kernel(own, other, weight, out):
    first = lax.axis_index("core") == 0
    half = own.shape[1]
    low = jnp.where(first, own[...], other[...]).astype(BF16)
    high = jnp.where(first, other[...], own[...]).astype(BF16)
    down = dot(low, weight[:half]) + dot(high, weight[half:])
    pieces = out.shape[0]
    width = down.shape[1] // pieces
    per_tile = LANES // width
    for piece in range(pieces):
        tile = down[:, piece // per_tile * LANES : (piece // per_tile + 1) * LANES]
        shift = piece % per_tile * width
        out[piece] = tile if shift == 0 else pltpu.roll(tile, LANES - shift, 1)


def finish_kernel(parts, carried, out):
    out[...] = carried[...] + jnp.sum(parts[...], axis=0)[:, : out.shape[1]]


VMEM = pl.BlockSpec(memory_space=pltpu.VMEM)
HBM = pl.BlockSpec(memory_space=pltpu.HBM)
WINDOW = pl.CostEstimate(flops=0, bytes_accessed=48 * 1024 * 1024, transcendentals=0)


def call(kernel, shapes, *args, specs=None, scratch=()):
    return pl.pallas_call(
        kernel,
        out_shape=shapes,
        in_specs=specs or [VMEM] * len(args),
        out_specs=jax.tree.map(lambda _: VMEM, shapes),
        scratch_shapes=scratch,
        cost_estimate=WINDOW,
        compiler_params=pltpu.CompilerParams(vmem_limit_bytes=16 * 1024 * 1024),
    )(*args)


def swap(array, axis):
    return lax.all_to_all(array, axis, split_axis=0, concat_axis=0, tiled=True)


def other_core(array):
    return lax.ppermute(array, "core", [(0, 1), (1, 0)])


def on_device(
    query,
    key_cache,
    value_cache,
    lengths,
    residual,
    out_weight,
    norm_gain,
    gate_weight,
    up_weight,
    down_weight,
):
    chips = lax.axis_size("chip")
    shards = chips * CORES
    groups = lax.axis_size("kvh")
    batch = query.shape[0]
    columns = norm_gain.shape[0]
    own = residual.shape[1]
    half = gate_weight.shape[1] // CORES
    padded = half + LANES

    def shape(*dims, dtype=F32):
        return jax.ShapeDtypeStruct(dims, dtype)

    keys = key_cache[:, :, 0, :]
    values = value_cache[:, :, 0, :]
    with jax.named_scope("attend"):
        ahead = (out_weight[0], up_weight, residual, norm_gain.reshape(1, columns))
        operands = [
            pltpu.with_memory_space_constraint(array, pltpu.HBM)
            for array in (lengths, query, keys, values, *ahead)
        ]
        partial, out_weight, up_weight, residual, gain = call(
            functools.partial(attend_kernel, batch),
            (
                shape(shards, batch, LANES),
                *(pltpu.VMEM(array.shape, array.dtype) for array in ahead),
            ),
            *operands,
            specs=[HBM] * len(operands),
            scratch=[
                pltpu.SMEM(lengths.shape, lengths.dtype),
                pltpu.VMEM(query.shape, query.dtype),
                pltpu.VMEM(keys.shape, keys.dtype),
                pltpu.VMEM(values.shape, values.dtype),
                pltpu.SemaphoreType.DMA((2 + 2 * batch + len(ahead),)),
            ],
        )
    partial = swap(partial, ("chip", "core"))
    with jax.named_scope("project"):
        projected = call(
            project_kernel,
            shape(shards, batch * columns // LANES, LANES, dtype=BF16),
            partial,
            out_weight,
        )
    projected = swap(projected, ("chip", "core"))
    with jax.named_scope("carry"):
        carried = call(carry_kernel, shape(groups, batch, columns), projected, residual)
    carried = swap(carried, "kvh")
    with jax.named_scope("gate_up"):
        keep, give, own_carried = call(
            gate_kernel,
            (shape(2 * batch, padded), shape(2 * batch, padded), shape(batch, own)),
            carried,
            gain,
            gate_weight,
            up_weight,
        )
    got = other_core(give)
    with jax.named_scope("pair"):
        hidden = call(pair_kernel, shape(chips, 4 * batch, padded // 2, dtype=BF16), keep, got)
    hidden = swap(hidden, "chip")
    with jax.named_scope("activate"):
        model_width = shards * columns
        activated = call(
            functools.partial(activate_kernel, model_width), shape(batch, half), hidden
        )
    other = other_core(activated)
    with jax.named_scope("down"):
        down = call(down_kernel, shape(groups, batch, LANES), activated, other, down_weight)
    down = swap(down, "kvh")
    with jax.named_scope("finish"):
        return call(finish_kernel, shape(batch, own), down, own_carried)


def solution(mesh):
    seq, kvh = mesh.devices.shape
    chips = Mesh(mesh.devices.reshape(seq // CORES, CORES, kvh), ("chip", "core", "kvh"))
    shard = ("chip", "core")
    return jax.shard_map(
        on_device,
        mesh=chips,
        in_specs=(
            P(None, "kvh", None),
            P(None, shard, "kvh", None),
            P(None, shard, "kvh", None),
            P(),
            P(None, (*shard, "kvh")),
            P("kvh", shard, None),
            P(shard),
            P(shard, "kvh"),
            P(shard, "kvh"),
            P("kvh", shard),
        ),
        out_specs=P(None, (*shard, "kvh")),
        check_vma=False,
    )
```

time: 90 us -> 76.1 us (0.85)
  blocking collectives: 77.1 us -> 63.9 us
  local copies, waits for them, and re-layouts: 7.85 us -> 0.01 us
  starting transfers between devices: 0 us -> 3.79 us
  waiting for transfers between devices: 0 us -> 1.74 us
  Pallas kernels: 4.6 us -> 6.31 us
    all_to_all x6 -> x5, blocking collectives: 77.1 us -> 63.9 us  [swap(): return lax.all_to_all(array, axis, split_axis=0, concat_axis=0, tiled=True)]
    unnamed x20 -> x4, local copies, waits for them, and re-layouts: 7.85 us -> 0.01 us
    ppermute x0 -> x2, starting transfers between devices: none -> 3.79 us  [other_core(): return lax.ppermute(array, 'core', [(0, 1), (1, 0)])]
    ppermute x0 -> x2, waiting for transfers between devices: none -> 1.74 us  [other_core(): return lax.ppermute(array, 'core', [(0, 1), (1, 0)])]
    pallas_call x7 -> x8, Pallas kernels: 4.6 us -> 6.31 us  [call(): pl.pallas_call(kernel, out_shape=shapes, in_specs=specs or [VMEM] * len(a...]
  transfers between devices with their start and end apart: 0 -> 2, of which waited for: 0 -> 2; matrix products, arithmetic and copies ran while one was open for 0% -> 0% of each run, Pallas kernels for 0% -> 0%
where the time goes in v2:
time: 76.1 us; the launch traced here: 75.8 us
  blocking collectives  63.9 us (84%)
  Pallas kernels  6.31 us (8%)
  starting transfers between devices  3.79 us (5%)
  waiting for transfers between devices  1.74 us (2%)
    all_to_all x5, blocking collectives, swap(): return lax.all_to_all(array, axis, split_axis=0, concat_axis=0, tiled=True)  63.9 us
    pallas_call x8, Pallas kernels, call(): pl.pallas_call(kernel, out_shape=shapes, in_specs=specs or [VMEM] * len(a...  6.31 us
    ppermute x2, starting transfers between devices, other_core(): return lax.ppermute(array, 'core', [(0, 1), (1, 0)])  3.79 us
    ppermute x2, waiting for transfers between devices, other_core(): return lax.ppermute(array, 'core', [(0, 1), (1, 0)])  1.74 us
  transfers between devices with their start and end apart: 2, of which 2 were waited for; matrix products, arithmetic and copies ran while one was open for 0% of the time, Pallas kernels for 0%

profile of v2, /device:TPU:1, one launch (start us, length us, event | category | flops | bytes accessed | tf_op | source)
XLA Modules:
  0.0 75.8 jit_solution(12031583370937511271)
XLA Ops:
  0.0 0.0 copy-start
  0.0 3.3 %attend.1 = (f32[32,4,128]{2,1,0:T(4,128)S(1)}, bf16[64,16384]{1,0:T(8,128)(2,1)S(1)}, bf16[512,3328]{1,0:T(8,128)(2,1)S(1)}, f32[4,64]{1,0:T(4,128)S(1)}, f32[1,512]{1,0:T(1,128)S(1)}) custom-call(s32[4]{0:T(128)} %refs_0_.1, bf16[4,16,128]{2,1,0:T(8,128)(2,1)} %refs_1_.1, bf16[4,512,128]{2,1,0:T(8,128)(2,1)} %bitcast.5, bf16[4,512,128]{2,1,0:T(8,128)(2,1)} %bitcast.6, ...), custom_call_target="tpu_custom_call" | custom-call | bytes 50331648 | tf_op jit(solution)/shard_map/attend/pallas_call | solution.py:198
  3.3 15.7 %all_to_all.25.parts = f32[32,4,128]{2,1,0:T(4,128)S(1)} all-to-all(f32[32,4,128]{2,1,0:T(4,128)S(1)} %get-tuple-element.13), channel_id=1, replica_groups=mesh['chip'=16,'core'=2,'kvh'=8] {'chip','core'}, dimensions={0} | all-to-all | bytes 131072 | tf_op jit(solution)/shard_map/all_to_all | solution.py:210
  19.0 0.6 project.1
  19.6 11.2 %all_to_all.26.parts = bf16[32,16,128]{2,1,0:T(8,128)(2,1)S(1)} all-to-all(bf16[32,16,128]{2,1,0:T(8,128)(2,1)S(1)} %project.1), channel_id=1, replica_groups=mesh['chip'=16,'core'=2,'kvh'=8] {'chip','core'}, dimensions={0} | all-to-all | bytes 262144 | tf_op jit(solution)/shard_map/all_to_all | solution.py:210
  30.8 0.1 carry.1
  30.9 15.2 %all_to_all.27.parts = f32[8,4,512]{2,1,0:T(4,128)S(1)} all-to-all(f32[8,4,512]{2,1,0:T(4,128)S(1)} %carry.1), channel_id=1, replica_groups=mesh['chip'=16,'core'=2,'kvh'=8] {'kvh'}, dimensions={0} | all-to-all | bytes 131072 | tf_op jit(solution)/shard_map/all_to_all | solution.py:210
  46.1 0.0 copy-done
  46.1 0.0 copy-start.1
  46.1 1.0 %gate_up.1 = (f32[8,1792]{1,0:T(8,128)S(1)}, f32[8,1792]{1,0:T(8,128)S(1)}, f32[4,64]{1,0:T(4,128)S(1)}) custom-call(f32[8,4,512]{2,1,0:T(4,128)S(1)} %all_to_all.27.parts, f32[1,512]{1,0:T(1,128)S(1)} %get-tuple-element.16.gain, bf16[512,3328]{1,0:T(8,128)(2,1)S(1)} %copy-done, bf16[512,3328]{1,0:T(8,128)(2,1)S(1)} %get-tuple-element.17.up_weight), custom_call_target="tpu_custom_call" | custom-call | bytes 50331648 | tf_op jit(solution)/shard_map/gate_up/pallas_call | solution.py:198
  47.1 1.9 %collective-permute-start = (f32[8,1792]{1,0:T(8,128)S(1)}, f32[8,1792]{1,0:T(8,128)S(1)}, u32[]{:S(2)}, u32[]{:S(2)}) collective-permute-start(f32[8,1792]{1,0:T(8,128)S(1)} %get-tuple-element.19), channel_id=1, source_target_pairs={{0,8},{8,0},{1,9},{9,1},{2,10},{10,2},{3,11},{11,3},{4,12},{12,4},... | collective-permute-start | bytes 172040 | tf_op jit(solution)/shard_map/ppermute | solution.py:214
  49.0 0.9 %collective-permute-done.got = f32[8,1792]{1,0:T(8,128)S(1)} collective-permute-done((f32[8,1792]{1,0:T(8,128)S(1)}, f32[8,1792]{1,0:T(8,128)S(1)}, u32[]{:S(2)}, u32[]{:S(2)}) %collective-permute-start) | collective-permute-done | bytes 57376 | tf_op jit(solution)/shard_map/ppermute | solution.py:214
  49.9 12.9 %all_to_all.28.parts = bf16[16,16,896]{2,1,0:T(8,128)(2,1)S(1)} all-to-all(bf16[16,16,896]{2,1,0:T(8,128)(2,1)S(1)} %pair.1), channel_id=1, replica_groups=mesh['chip'=16,'core'=2,'kvh'=8] {'chip'}, dimensions={0} | all-to-all | bytes 917504 | tf_op jit(solution)/shard_map/all_to_all | solution.py:210
  62.8 0.1 activate.1.own
  62.9 1.9 %collective-permute-start.1 = (f32[4,1664]{1,0:T(4,128)S(1)}, f32[4,1664]{1,0:T(4,128)S(1)}, u32[]{:S(2)}, u32[]{:S(2)}) collective-permute-start(f32[4,1664]{1,0:T(4,128)S(1)} %activate.1.own), channel_id=1, source_target_pairs={{0,8},{8,0},{1,9},{9,1},{2,10},{10,2},{3,11},{11,3},{4,12},{12,4},... | collective-permute-start | bytes 79880 | tf_op jit(solution)/shard_map/ppermute | solution.py:214
  64.8 0.9 %collective-permute-done.1.other = f32[4,1664]{1,0:T(4,128)S(1)} collective-permute-done((f32[4,1664]{1,0:T(4,128)S(1)}, f32[4,1664]{1,0:T(4,128)S(1)}, u32[]{:S(2)}, u32[]{:S(2)}) %collective-permute-start.1) | collective-permute-done | bytes 26656 | tf_op jit(solution)/shard_map/ppermute | solution.py:214
  65.6 0.0 copy-done.1
  65.6 0.6 down.1
  66.3 9.0 %all_to_all.29.parts = f32[8,4,128]{2,1,0:T(4,128)S(1)} all-to-all(f32[8,4,128]{2,1,0:T(4,128)S(1)} %down.1), channel_id=1, replica_groups=mesh['chip'=16,'core'=2,'kvh'=8] {'kvh'}, dimensions={0} | all-to-all | bytes 32768 | tf_op jit(solution)/shard_map/all_to_all | solution.py:210
  75.2 0.6 finish.1
  (1 shorter events, 0.0 us)
Async XLA Ops:
  0.0 46.1 %copy-start = (bf16[512,3328]{1,0:T(8,128)(2,1)S(1)}, bf16[512,3328]{1,0:T(8,128)(2,1)}, u32[]{:S(2)}) copy-start(bf16[512,3328]{1,0:T(8,128)(2,1)} %gate_weight.1) | copy-start | bytes 10223620
  46.1 19.6 %copy-start.1 = (bf16[3328,512]{1,0:T(8,128)(2,1)S(1)}, bf16[3328,512]{1,0:T(8,128)(2,1)}, u32[]{:S(2)}) copy-start(bf16[3328,512]{1,0:T(8,128)(2,1)} %weight.1) | copy-start | bytes 10223620
  47.1 2.8 %collective-permute-start = (f32[8,1792]{1,0:T(8,128)S(1)}, f32[8,1792]{1,0:T(8,128)S(1)}, u32[]{:S(2)}, u32[]{:S(2)}) collective-permute-start(f32[8,1792]{1,0:T(8,128)S(1)} %get-tuple-element.19), channel_id=1, source_target_pairs={{0,8},{8,0},{1,9},{9,1},{2,10},{10,2},{3,11},{11,3},{4,12},{12,4},... | collective-permute-start | bytes 172040 | tf_op jit(solution)/shard_map/ppermute | solution.py:214
  62.9 2.7 %collective-permute-start.1 = (f32[4,1664]{1,0:T(4,128)S(1)}, f32[4,1664]{1,0:T(4,128)S(1)}, u32[]{:S(2)}, u32[]{:S(2)}) collective-permute-start(f32[4,1664]{1,0:T(4,128)S(1)} %activate.1.own), channel_id=1, source_target_pairs={{0,8},{8,0},{1,9},{9,1},{2,10},{10,2},{3,11},{11,3},{4,12},{12,4},... | collective-permute-start | bytes 79880 | tf_op jit(solution)/shard_map/ppermute | solution.py:214

commit v3 on v2

--- a/solution.py
+++ b/solution.py
@@ -45,10 +45,7 @@
         value_loads.append(pltpu.make_async_copy(values_hbm.at[b], values.at[b], sems.at[3 + 2 * b]))
     for load in loads:
         load.start()
-    for b in range(batch):
-        key_loads[b].start()
-        value_loads[b].start()
-    for load in later:
+    for load in key_loads + value_loads + later:
         load.start()
     for load in loads:
         load.wait()
@@ -58,31 +55,36 @@
     stat = (LANES - width) // 2
     shard = lax.axis_index("chip") * CORES + lax.axis_index("core")
     positions = shard * positions_here + lax.broadcasted_iota(jnp.int32, (heads, positions_here), 1)
+    weights, tops, totals = [], [], []
+    for load in key_loads:
+        load.wait()
     for b in range(batch):
-        key_loads[b].wait()
         scores = lax.dot_general(
             query[b], keys[b], (((1,), (1,)), ((), ())), preferred_element_type=F32
         ) * head_dim ** (-0.5)
         live = positions < lengths[b]
         masked = jnp.where(live, scores, MASKED)
         top = jnp.max(masked, axis=1, keepdims=True)
-        weights = jnp.where(live, jnp.exp(masked - top), 0.0)
-        total = jnp.sum(weights, axis=1, keepdims=True)
-        value_loads[b].wait()
-        both = dot(jnp.concatenate(split(weights), axis=0), values[b])
+        weights.append(jnp.where(live, jnp.exp(masked - top), 0.0))
+        tops.append(jnp.broadcast_to(top, (heads, stat)))
+        totals.append(jnp.broadcast_to(jnp.sum(weights[b], axis=1, keepdims=True), (heads, stat)))
+    for load in value_loads:
+        load.wait()
+    for b in range(batch):
+        both = dot(jnp.concatenate(split(weights[b]), axis=0), values[b])
         sums = both[:heads] + both[heads:]
-        stats = jnp.concatenate(
-            [jnp.broadcast_to(top, (heads, stat)), jnp.broadcast_to(total, (heads, stat))], axis=1
-        )
         for part in range(per_head):
-            packed = jnp.concatenate([sums[:, part * width : (part + 1) * width], stats], axis=1)
+            packed = jnp.concatenate(
+                [sums[:, part * width : (part + 1) * width], tops[b], totals[b]], axis=1
+            )
             for h in range(heads):
                 out[h * per_head + part, b : b + 1, :] = packed[h : h + 1]
     for load in later:
         load.wait()
 
 
-def project_kernel(parts, weight, out):
+def project_kernel(parts, weight, *refs):
+    out = refs[-1]
     width = weight.shape[0]
     stat = (LANES - width) // 2
     got = parts[...]
@@ -118,7 +120,17 @@
         out[piece] = summed
 
 
-def gate_kernel(parts, gain, gate_weight, up_weight, keep, give, carried_out):
+def gate_up_half(scaled, core, gate_weight, up_weight):
+    batch = scaled.shape[0]
+    terms = jnp.concatenate(split(scaled), axis=0)
+    half = gate_weight.shape[1] // CORES
+    lanes = pl.ds(pl.multiple_of(core * half, LANES), half)
+    gate = dot(terms, gate_weight[:, lanes])
+    up = dot(terms, up_weight[:, lanes])
+    return jnp.concatenate([gate[:batch] + gate[batch:], up[:batch] + up[batch:]], axis=0)
+
+
+def gate_give_kernel(parts, gain, gate_weight, up_weight, give, scaled_out, squares_out, carried_out):
     batch = parts.shape[1]
     carried = jnp.sum(parts[...], axis=0)
     width = carried_out.shape[1]
@@ -127,20 +139,19 @@
         own[:, piece * width : (piece + 1) * width] for piece in range(carried.shape[1] // width)
     )
     squares = jnp.sum(carried * carried, axis=1, keepdims=True)
-    terms = jnp.concatenate(split(carried * gain[...]), axis=0)
+    squares = jnp.broadcast_to(jnp.concatenate([squares, squares], axis=0), (2 * batch, LANES))
+    scaled = carried * gain[...]
     half = gate_weight.shape[1] // CORES
-    first = lax.axis_index("core") == 0
-    halves = []
-    for core in range(CORES):
-        lanes = slice(core * half, (core + 1) * half)
-        gate = dot(terms, gate_weight[:, lanes])
-        up = dot(terms, up_weight[:, lanes])
-        halves.append(jnp.concatenate([gate[:batch] + gate[batch:], up[:batch] + up[batch:]], axis=0))
-    keep[:, :half] = jnp.where(first, halves[0], halves[1])
-    give[:, :half] = jnp.where(first, halves[1], halves[0])
-    squares = jnp.broadcast_to(jnp.concatenate([squares, squares], axis=0), (2 * batch, LANES))
-    keep[:, half:] = squares
+    give[:, :half] = gate_up_half(scaled, 1 - lax.axis_index("core"), gate_weight, up_weight)
     give[:, half:] = squares
+    scaled_out[...] = scaled
+    squares_out[...] = squares
+
+
+def gate_keep_kernel(scaled, squares, gate_weight, up_weight, keep):
+    half = gate_weight.shape[1] // CORES
+    keep[:, :half] = gate_up_half(scaled[...], lax.axis_index("core"), gate_weight, up_weight)
+    keep[:, half:] = squares[...]
 
 
 def pair_kernel(keep, got, out):
@@ -170,12 +181,18 @@
     out[...] = (gate / (1.0 + jnp.exp(-gate)) * up).astype(BF16).astype(F32)
 
 
-def down_kernel(own, other, weight, out):
-    first = lax.axis_index("core") == 0
-    half = own.shape[1]
-    low = jnp.where(first, own[...], other[...]).astype(BF16)
-    high = jnp.where(first, other[...], own[...]).astype(BF16)
-    down = dot(low, weight[:half]) + dot(high, weight[half:])
+def down_half(activated, core, weight):
+    half = weight.shape[0] // CORES
+    rows = pl.ds(pl.multiple_of(core * half, LANES), half)
+    return dot(activated[...].astype(BF16), weight[rows, :])
+
+
+def down_own_kernel(activated, weight, out):
+    out[...] = down_half(activated, lax.axis_index("core"), weight)
+
+
+def down_kernel(activated, weight, own, out):
+    down = own[...] + down_half(activated, 1 - lax.axis_index("core"), weight)
     pieces = out.shape[0]
     width = down.shape[1] // pieces
     per_tile = LANES // width
@@ -191,7 +208,7 @@
 
 VMEM = pl.BlockSpec(memory_space=pltpu.VMEM)
 HBM = pl.BlockSpec(memory_space=pltpu.HBM)
-WINDOW = pl.CostEstimate(flops=0, bytes_accessed=48 * 1024 * 1024, transcendentals=0)
+SHORT = pl.CostEstimate(flops=0, bytes_accessed=2 * 1024 * 1024, transcendentals=0)
 
 
 def call(kernel, shapes, *args, specs=None, scratch=()):
@@ -201,7 +218,7 @@
         in_specs=specs or [VMEM] * len(args),
         out_specs=jax.tree.map(lambda _: VMEM, shapes),
         scratch_shapes=scratch,
-        cost_estimate=WINDOW,
+        cost_estimate=SHORT,
         compiler_params=pltpu.CompilerParams(vmem_limit_bytes=16 * 1024 * 1024),
     )(*args)
 
@@ -241,12 +258,12 @@
     keys = key_cache[:, :, 0, :]
     values = value_cache[:, :, 0, :]
     with jax.named_scope("attend"):
-        ahead = (out_weight[0], up_weight, residual, norm_gain.reshape(1, columns))
+        ahead = (out_weight[0], residual, norm_gain.reshape(1, columns))
         operands = [
             pltpu.with_memory_space_constraint(array, pltpu.HBM)
             for array in (lengths, query, keys, values, *ahead)
         ]
-        partial, out_weight, up_weight, residual, gain = call(
+        partial, out_weight, residual, gain = call(
             functools.partial(attend_kernel, batch),
             (
                 shape(shards, batch, LANES),
@@ -269,21 +286,35 @@
             shape(shards, batch * columns // LANES, LANES, dtype=BF16),
             partial,
             out_weight,
+            *(
+                pltpu.with_memory_space_constraint(array, pltpu.HBM)
+                for array in (gate_weight, up_weight, down_weight)
+            ),
+            specs=[VMEM] * 2 + [HBM] * 3,
         )
     projected = swap(projected, ("chip", "core"))
     with jax.named_scope("carry"):
         carried = call(carry_kernel, shape(groups, batch, columns), projected, residual)
     carried = swap(carried, "kvh")
-    with jax.named_scope("gate_up"):
-        keep, give, own_carried = call(
-            gate_kernel,
-            (shape(2 * batch, padded), shape(2 * batch, padded), shape(batch, own)),
+    with jax.named_scope("gate_up_give"):
+        give, scaled, squares, own_carried = call(
+            gate_give_kernel,
+            (
+                shape(2 * batch, padded),
+                shape(batch, columns),
+                shape(2 * batch, LANES),
+                shape(batch, own),
+            ),
             carried,
             gain,
             gate_weight,
             up_weight,
         )
     got = other_core(give)
+    with jax.named_scope("gate_up_keep"):
+        keep = call(
+            gate_keep_kernel, shape(2 * batch, padded), scaled, squares, gate_weight, up_weight
+        )
     with jax.named_scope("pair"):
         hidden = call(pair_kernel, shape(chips, 4 * batch, padded // 2, dtype=BF16), keep, got)
     hidden = swap(hidden, "chip")
@@ -293,8 +324,10 @@
             functools.partial(activate_kernel, model_width), shape(batch, half), hidden
         )
     other = other_core(activated)
+    with jax.named_scope("down_own"):
+        down = call(down_own_kernel, shape(batch, columns), activated, down_weight)
     with jax.named_scope("down"):
-        down = call(down_kernel, shape(groups, batch, LANES), activated, other, down_weight)
+        down = call(down_kernel, shape(groups, batch, LANES), other, down_weight, down)
     down = swap(down, "kvh")
     with jax.named_scope("finish"):
         return call(finish_kernel, shape(batch, own), down, own_carried)

time: 76.1 us -> 74.7 us (0.982)
  Pallas kernels: 6.31 us -> 5.4 us
  waiting for transfers between devices: 1.74 us -> 0.85 us
    pallas_call x8 -> x10, Pallas kernels: 6.31 us -> 5.4 us  [call(): pl.pallas_call(kernel, out_shape=shapes, in_specs=specs or [VMEM] * len(a...]
    ppermute x2, waiting for transfers between devices: 1.74 us -> 0.85 us  [other_core(): return lax.ppermute(array, 'core', [(0, 1), (1, 0)])]
  transfers between devices with their start and end apart: 2 -> 2, of which waited for: 2 -> 2; matrix products, arithmetic and copies ran while one was open for 0% -> 0% of each run, Pallas kernels for 0% -> 1%
where the time goes in v3:
time: 74.7 us; the launch traced here: 74.4 us
  blocking collectives  64.5 us (86%)
  Pallas kernels  5.4 us (7%)
  starting transfers between devices  3.64 us (5%)
  waiting for transfers between devices  0.85 us (1%)
    all_to_all x5, blocking collectives, swap(): return lax.all_to_all(array, axis, split_axis=0, concat_axis=0, tiled=True)  64.5 us
    pallas_call x10, Pallas kernels, call(): pl.pallas_call(kernel, out_shape=shapes, in_specs=specs or [VMEM] * len(a...  5.4 us
    ppermute x2, starting transfers between devices, other_core(): return lax.ppermute(array, 'core', [(0, 1), (1, 0)])  3.64 us
  transfers between devices with their start and end apart: 2, of which 2 were waited for; matrix products, arithmetic and copies ran while one was open for 0% of the time, Pallas kernels for 1%

profile of v3, /device:TPU:1, one launch (start us, length us, event | category | flops | bytes accessed | tf_op | source)
XLA Modules:
  0.0 74.4 jit_solution(7508601141645243112)
XLA Ops:
  0.0 2.2 %attend.1 = (f32[32,4,128]{2,1,0:T(4,128)S(1)}, bf16[64,16384]{1,0:T(8,128)(2,1)S(1)}, f32[4,64]{1,0:T(4,128)S(1)}, f32[1,512]{1,0:T(1,128)S(1)}) custom-call(s32[4]{0:T(128)} %refs_0_.2, bf16[4,16,128]{2,1,0:T(8,128)(2,1)} %refs_1_.2, bf16[4,512,128]{2,1,0:T(8,128)(2,1)} %bitcast.5, bf16[4,512,128]{2,1,0:T(8,128)(2,1)} %bitcast.6, ...), custom_call_target="tpu_custom_call" | custom-call | bytes 2097152 | tf_op jit(solution)/shard_map/attend/pallas_call | solution.py:215
  2.2 15.7 %all_to_all.25.parts = f32[32,4,128]{2,1,0:T(4,128)S(1)} all-to-all(f32[32,4,128]{2,1,0:T(4,128)S(1)} %get-tuple-element.13), channel_id=1, replica_groups=mesh['chip'=16,'core'=2,'kvh'=8] {'chip','core'}, dimensions={0} | all-to-all | bytes 131072 | tf_op jit(solution)/shard_map/all_to_all | solution.py:227
  17.9 0.0 copy-start
  17.9 0.0 copy-start.1
  17.9 0.6 project.1
  18.4 11.4 %all_to_all.26.parts = bf16[32,16,128]{2,1,0:T(8,128)(2,1)S(1)} all-to-all(bf16[32,16,128]{2,1,0:T(8,128)(2,1)S(1)} %project.1), channel_id=1, replica_groups=mesh['chip'=16,'core'=2,'kvh'=8] {'chip','core'}, dimensions={0} | all-to-all | bytes 262144 | tf_op jit(solution)/shard_map/all_to_all | solution.py:227
  29.9 0.1 carry.1
  30.0 15.2 %all_to_all.27.parts = f32[8,4,512]{2,1,0:T(4,128)S(1)} all-to-all(f32[8,4,512]{2,1,0:T(4,128)S(1)} %carry.1), channel_id=1, replica_groups=mesh['chip'=16,'core'=2,'kvh'=8] {'kvh'}, dimensions={0} | all-to-all | bytes 131072 | tf_op jit(solution)/shard_map/all_to_all | solution.py:227
  45.2 0.0 copy-done
  45.2 0.0 copy-done.1
  45.2 0.6 gate_up_give.1
  45.7 1.9 %collective-permute-start = (f32[8,1792]{1,0:T(8,128)S(1)}, f32[8,1792]{1,0:T(8,128)S(1)}, u32[]{:S(2)}, u32[]{:S(2)}) collective-permute-start(f32[8,1792]{1,0:T(8,128)S(1)} %get-tuple-element.19), channel_id=1, source_target_pairs={{0,8},{8,0},{1,9},{9,1},{2,10},{10,2},{3,11},{11,3},{4,12},{12,4},... | collective-permute-start | bytes 172040 | tf_op jit(solution)/shard_map/ppermute | solution.py:231
  47.7 0.0 copy-start.2
  47.7 0.6 gate_up_keep.1.keep
  48.2 0.3 collective-permute-done.got
  48.6 13.1 %all_to_all.28.parts = bf16[16,16,896]{2,1,0:T(8,128)(2,1)S(1)} all-to-all(bf16[16,16,896]{2,1,0:T(8,128)(2,1)S(1)} %pair.1), channel_id=1, replica_groups=mesh['chip'=16,'core'=2,'kvh'=8] {'chip'}, dimensions={0} | all-to-all | bytes 917504 | tf_op jit(solution)/shard_map/all_to_all | solution.py:227
  61.7 0.1 activate.1.activated
  61.9 1.7 %collective-permute-start.1 = (f32[4,1664]{1,0:T(4,128)S(1)}, f32[4,1664]{1,0:T(4,128)S(1)}, u32[]{:S(2)}, u32[]{:S(2)}) collective-permute-start(f32[4,1664]{1,0:T(4,128)S(1)} %activate.1.activated), channel_id=1, source_target_pairs={{0,8},{8,0},{1,9},{9,1},{2,10},{10,2},{3,11},{11,3},{4,12},{12,4},... | collective-permute-start | bytes 79880 | tf_op jit(solution)/shard_map/ppermute | solution.py:231
  63.6 0.0 copy-done.2
  63.6 0.3 down_own.1.own
  63.9 0.5 collective-permute-done.1.activated
  64.4 0.4 down.1
  64.8 9.0 %all_to_all.29.parts = f32[8,4,128]{2,1,0:T(4,128)S(1)} all-to-all(f32[8,4,128]{2,1,0:T(4,128)S(1)} %down.1), channel_id=1, replica_groups=mesh['chip'=16,'core'=2,'kvh'=8] {'kvh'}, dimensions={0} | all-to-all | bytes 32768 | tf_op jit(solution)/shard_map/all_to_all | solution.py:227
  73.8 0.6 finish.1
  (1 shorter events, 0.0 us)
Async XLA Ops:
  17.9 27.3 %copy-start = (bf16[512,3328]{1,0:T(8,128)(2,1)S(1)}, bf16[512,3328]{1,0:T(8,128)(2,1)}, u32[]{:S(2)}) copy-start(bf16[512,3328]{1,0:T(8,128)(2,1)} %gate_weight.3) | copy-start | bytes 10223620
  17.9 27.3 %copy-start.1 = (bf16[512,3328]{1,0:T(8,128)(2,1)S(1)}, bf16[512,3328]{1,0:T(8,128)(2,1)}, u32[]{:S(2)}) copy-start(bf16[512,3328]{1,0:T(8,128)(2,1)} %up_weight.3) | copy-start | bytes 10223620
  45.7 2.8 %collective-permute-start = (f32[8,1792]{1,0:T(8,128)S(1)}, f32[8,1792]{1,0:T(8,128)S(1)}, u32[]{:S(2)}, u32[]{:S(2)}) collective-permute-start(f32[8,1792]{1,0:T(8,128)S(1)} %get-tuple-element.19), channel_id=1, source_target_pairs={{0,8},{8,0},{1,9},{9,1},{2,10},{10,2},{3,11},{11,3},{4,12},{12,4},... | collective-permute-start | bytes 172040 | tf_op jit(solution)/shard_map/ppermute | solution.py:231
  47.7 15.9 %copy-start.2 = (bf16[3328,512]{1,0:T(8,128)(2,1)S(1)}, bf16[3328,512]{1,0:T(8,128)(2,1)}, u32[]{:S(2)}) copy-start(bf16[3328,512]{1,0:T(8,128)(2,1)} %weight.3) | copy-start | bytes 10223620
  61.9 2.6 %collective-permute-start.1 = (f32[4,1664]{1,0:T(4,128)S(1)}, f32[4,1664]{1,0:T(4,128)S(1)}, u32[]{:S(2)}, u32[]{:S(2)}) collective-permute-start(f32[4,1664]{1,0:T(4,128)S(1)} %activate.1.activated), channel_id=1, source_target_pairs={{0,8},{8,0},{1,9},{9,1},{2,10},{10,2},{3,11},{11,3},{4,12},{12,4},... | collective-permute-start | bytes 79880 | tf_op jit(solution)/shard_map/ppermute | solution.py:231

commit v4 on v3

--- a/solution.py
+++ b/solution.py
@@ -26,11 +26,11 @@
 
 def attend_kernel(batch, *refs):
     lengths_hbm, query_hbm, keys_hbm, values_hbm = refs[:4]
-    ahead = (len(refs) - 10) // 2
-    out = refs[4 + ahead]
+    ahead = (len(refs) - 14) // 2
+    out = refs[8 + ahead]
     lengths, query, keys, values, sems = refs[-5:]
     later = [
-        pltpu.make_async_copy(refs[4 + i], refs[5 + ahead + i], sems.at[2 + 2 * batch + i])
+        pltpu.make_async_copy(refs[4 + i], refs[9 + ahead + i], sems.at[4 + i])
         for i in range(ahead)
     ]
     heads, head_dim = query.shape[1:]
@@ -39,13 +39,9 @@
         pltpu.make_async_copy(lengths_hbm, lengths, sems.at[0]),
         pltpu.make_async_copy(query_hbm, query, sems.at[1]),
     ]
-    key_loads, value_loads = [], []
-    for b in range(batch):
-        key_loads.append(pltpu.make_async_copy(keys_hbm.at[b], keys.at[b], sems.at[2 + 2 * b]))
-        value_loads.append(pltpu.make_async_copy(values_hbm.at[b], values.at[b], sems.at[3 + 2 * b]))
-    for load in loads:
-        load.start()
-    for load in key_loads + value_loads + later:
+    key_load = pltpu.make_async_copy(keys_hbm, keys, sems.at[2])
+    value_load = pltpu.make_async_copy(values_hbm, values, sems.at[3])
+    for load in (*loads, key_load, value_load, *later):
         load.start()
     for load in loads:
         load.wait()
@@ -56,8 +52,7 @@
     shard = lax.axis_index("chip") * CORES + lax.axis_index("core")
     positions = shard * positions_here + lax.broadcasted_iota(jnp.int32, (heads, positions_here), 1)
     weights, tops, totals = [], [], []
-    for load in key_loads:
-        load.wait()
+    key_load.wait()
     for b in range(batch):
         scores = lax.dot_general(
             query[b], keys[b], (((1,), (1,)), ((), ())), preferred_element_type=F32
@@ -68,8 +63,7 @@
         weights.append(jnp.where(live, jnp.exp(masked - top), 0.0))
         tops.append(jnp.broadcast_to(top, (heads, stat)))
         totals.append(jnp.broadcast_to(jnp.sum(weights[b], axis=1, keepdims=True), (heads, stat)))
-    for load in value_loads:
-        load.wait()
+    value_load.wait()
     for b in range(batch):
         both = dot(jnp.concatenate(split(weights[b]), axis=0), values[b])
         sums = both[:heads] + both[heads:]
@@ -83,8 +77,7 @@
         load.wait()
 
 
-def project_kernel(parts, weight, *refs):
-    out = refs[-1]
+def project_kernel(parts, weight, out):
     width = weight.shape[0]
     stat = (LANES - width) // 2
     got = parts[...]
@@ -130,7 +123,9 @@
     return jnp.concatenate([gate[:batch] + gate[batch:], up[:batch] + up[batch:]], axis=0)
 
 
-def gate_give_kernel(parts, gain, gate_weight, up_weight, give, scaled_out, squares_out, carried_out):
+def gate_give_kernel(
+    parts, gain, gate_weight, up_weight, _, give, scaled_out, squares_out, carried_out
+):
     batch = parts.shape[1]
     carried = jnp.sum(parts[...], axis=0)
     width = carried_out.shape[1]
@@ -258,12 +253,12 @@
     keys = key_cache[:, :, 0, :]
     values = value_cache[:, :, 0, :]
     with jax.named_scope("attend"):
-        ahead = (out_weight[0], residual, norm_gain.reshape(1, columns))
+        ahead = (residual, norm_gain.reshape(1, columns))
         operands = [
             pltpu.with_memory_space_constraint(array, pltpu.HBM)
-            for array in (lengths, query, keys, values, *ahead)
+            for array in (lengths, query, keys, values, *ahead, out_weight, gate_weight, up_weight, down_weight)
         ]
-        partial, out_weight, residual, gain = call(
+        partial, residual, gain = call(
             functools.partial(attend_kernel, batch),
             (
                 shape(shards, batch, LANES),
@@ -276,7 +271,7 @@
                 pltpu.VMEM(query.shape, query.dtype),
                 pltpu.VMEM(keys.shape, keys.dtype),
                 pltpu.VMEM(values.shape, values.dtype),
-                pltpu.SemaphoreType.DMA((2 + 2 * batch + len(ahead),)),
+                pltpu.SemaphoreType.DMA((4 + len(ahead),)),
             ],
         )
     partial = swap(partial, ("chip", "core"))
@@ -285,12 +280,7 @@
             project_kernel,
             shape(shards, batch * columns // LANES, LANES, dtype=BF16),
             partial,
-            out_weight,
-            *(
-                pltpu.with_memory_space_constraint(array, pltpu.HBM)
-                for array in (gate_weight, up_weight, down_weight)
-            ),
-            specs=[VMEM] * 2 + [HBM] * 3,
+            out_weight[0],
         )
     projected = swap(projected, ("chip", "core"))
     with jax.named_scope("carry"):
@@ -309,6 +299,7 @@
             gain,
             gate_weight,
             up_weight,
+            down_weight,
         )
     got = other_core(give)
     with jax.named_scope("gate_up_keep"):

time: 74.7 us -> 74.4 us (level)
  no operation moved by 1% of the time
where the time goes in v4:
time: 74.4 us; the launch traced here: 74.1 us
  blocking collectives  64.2 us (86%)
  Pallas kernels  5.2 us (7%)
  starting transfers between devices  3.79 us (5%)
  waiting for transfers between devices  0.85 us (1%)
    all_to_all x5, blocking collectives, swap(): return lax.all_to_all(array, axis, split_axis=0, concat_axis=0, tiled=True)  64.2 us
    pallas_call x10, Pallas kernels, call(): pl.pallas_call(kernel, out_shape=shapes, in_specs=specs or [VMEM] * len(a...  5.2 us
    ppermute x2, starting transfers between devices, other_core(): return lax.ppermute(array, 'core', [(0, 1), (1, 0)])  3.79 us
  transfers between devices with their start and end apart: 2, of which 2 were waited for; matrix products, arithmetic and copies ran while one was open for 0% of the time, Pallas kernels for 1%

profile of v4, /device:TPU:1, one launch (start us, length us, event | category | flops | bytes accessed | tf_op | source)
XLA Modules:
  0.0 74.1 jit_solution(11756383030059765696)
XLA Ops:
  0.0 0.0 copy-start.3
  0.0 0.0 copy-start
  0.0 0.0 copy-start.1
  0.0 0.0 copy-start.2
  0.0 2.0 %attend.1 = (f32[32,4,128]{2,1,0:T(4,128)S(1)}, f32[4,64]{1,0:T(4,128)S(1)}, f32[1,512]{1,0:T(1,128)S(1)}) custom-call(s32[4]{0:T(128)} %refs_0_.1, bf16[4,16,128]{2,1,0:T(8,128)(2,1)} %refs_1_.1, bf16[4,512,128]{2,1,0:T(8,128)(2,1)} %bitcast.5, bf16[4,512,128]{2,1,0:T(8,128)(2,1)} %bitcast.6, f32[4,64]{1,0:T(4,128)} %refs_4_.1, f32[1,512]{1,0:T(1,128)} %bitcast.7, ...), custom_call_target="tpu_custom_call" | custom-call | bytes 2097152 | tf_op jit(solution)/shard_map/attend/pallas_call | solution.py:210
  2.0 16.0 %all_to_all.25.parts = f32[32,4,128]{2,1,0:T(4,128)S(1)} all-to-all(f32[32,4,128]{2,1,0:T(4,128)S(1)} %get-tuple-element.12), channel_id=1, replica_groups=mesh['chip'=16,'core'=2,'kvh'=8] {'chip','core'}, dimensions={0} | all-to-all | bytes 131072 | tf_op jit(solution)/shard_map/all_to_all | solution.py:222
  18.0 0.0 copy-done.3
  18.0 0.6 project.1
  18.5 11.2 %all_to_all.26.parts = bf16[32,16,128]{2,1,0:T(8,128)(2,1)S(1)} all-to-all(bf16[32,16,128]{2,1,0:T(8,128)(2,1)S(1)} %project.1), channel_id=1, replica_groups=mesh['chip'=16,'core'=2,'kvh'=8] {'chip','core'}, dimensions={0} | all-to-all | bytes 262144 | tf_op jit(solution)/shard_map/all_to_all | solution.py:222
  29.7 0.1 carry.1
  29.8 15.2 %all_to_all.27.parts = f32[8,4,512]{2,1,0:T(4,128)S(1)} all-to-all(f32[8,4,512]{2,1,0:T(4,128)S(1)} %carry.1), channel_id=1, replica_groups=mesh['chip'=16,'core'=2,'kvh'=8] {'kvh'}, dimensions={0} | all-to-all | bytes 131072 | tf_op jit(solution)/shard_map/all_to_all | solution.py:222
  45.0 0.0 copy-done
  45.0 0.0 copy-done.1
  45.0 0.0 copy-done.2
  45.0 0.6 gate_up_give.1
  45.6 1.9 %collective-permute-start = (f32[8,1792]{1,0:T(8,128)S(1)}, f32[8,1792]{1,0:T(8,128)S(1)}, u32[]{:S(2)}, u32[]{:S(2)}) collective-permute-start(f32[8,1792]{1,0:T(8,128)S(1)} %get-tuple-element.17), channel_id=1, source_target_pairs={{0,8},{8,0},{1,9},{9,1},{2,10},{10,2},{3,11},{11,3},{4,12},{12,4},... | collective-permute-start | bytes 172040 | tf_op jit(solution)/shard_map/ppermute | solution.py:226
  47.5 0.6 gate_up_keep.1.keep
  48.0 0.3 collective-permute-done.got
  48.4 12.9 %all_to_all.28.parts = bf16[16,16,896]{2,1,0:T(8,128)(2,1)S(1)} all-to-all(bf16[16,16,896]{2,1,0:T(8,128)(2,1)S(1)} %pair.1), channel_id=1, replica_groups=mesh['chip'=16,'core'=2,'kvh'=8] {'chip'}, dimensions={0} | all-to-all | bytes 917504 | tf_op jit(solution)/shard_map/all_to_all | solution.py:222
  61.3 0.1 activate.1.activated
  61.4 1.9 %collective-permute-start.1 = (f32[4,1664]{1,0:T(4,128)S(1)}, f32[4,1664]{1,0:T(4,128)S(1)}, u32[]{:S(2)}, u32[]{:S(2)}) collective-permute-start(f32[4,1664]{1,0:T(4,128)S(1)} %activate.1.activated), channel_id=1, source_target_pairs={{0,8},{8,0},{1,9},{9,1},{2,10},{10,2},{3,11},{11,3},{4,12},{12,4},... | collective-permute-start | bytes 79880 | tf_op jit(solution)/shard_map/ppermute | solution.py:226
  63.3 0.3 down_own.1.own
  63.6 0.5 collective-permute-done.1.activated
  64.1 0.4 down.1
  64.5 9.0 %all_to_all.29.parts = f32[8,4,128]{2,1,0:T(4,128)S(1)} all-to-all(f32[8,4,128]{2,1,0:T(4,128)S(1)} %down.1), channel_id=1, replica_groups=mesh['chip'=16,'core'=2,'kvh'=8] {'kvh'}, dimensions={0} | all-to-all | bytes 32768 | tf_op jit(solution)/shard_map/all_to_all | solution.py:222
  73.5 0.6 finish.1
  (1 shorter events, 0.0 us)
Async XLA Ops:
  0.0 18.0 %copy-start.3 = (bf16[1,64,16384]{2,1,0:T(8,128)(2,1)S(1)}, bf16[1,64,16384]{2,1,0:T(8,128)(2,1)}, u32[]{:S(2)}) copy-start(bf16[1,64,16384]{2,1,0:T(8,128)(2,1)} %refs_6_.1) | copy-start | bytes 6291460
  0.0 45.0 %copy-start = (bf16[3328,512]{1,0:T(8,128)(2,1)S(1)}, bf16[3328,512]{1,0:T(8,128)(2,1)}, u32[]{:S(2)}) copy-start(bf16[3328,512]{1,0:T(8,128)(2,1)} %weight.3) | copy-start | bytes 10223620
  0.0 45.0 %copy-start.1 = (bf16[512,3328]{1,0:T(8,128)(2,1)S(1)}, bf16[512,3328]{1,0:T(8,128)(2,1)}, u32[]{:S(2)}) copy-start(bf16[512,3328]{1,0:T(8,128)(2,1)} %gate_weight.3) | copy-start | bytes 10223620
  0.0 45.0 %copy-start.2 = (bf16[512,3328]{1,0:T(8,128)(2,1)S(1)}, bf16[512,3328]{1,0:T(8,128)(2,1)}, u32[]{:S(2)}) copy-start(bf16[512,3328]{1,0:T(8,128)(2,1)} %up_weight.3) | copy-start | bytes 10223620
  45.6 2.8 %collective-permute-start = (f32[8,1792]{1,0:T(8,128)S(1)}, f32[8,1792]{1,0:T(8,128)S(1)}, u32[]{:S(2)}, u32[]{:S(2)}) collective-permute-start(f32[8,1792]{1,0:T(8,128)S(1)} %get-tuple-element.17), channel_id=1, source_target_pairs={{0,8},{8,0},{1,9},{9,1},{2,10},{10,2},{3,11},{11,3},{4,12},{12,4},... | collective-permute-start | bytes 172040 | tf_op jit(solution)/shard_map/ppermute | solution.py:226
  61.4 2.7 %collective-permute-start.1 = (f32[4,1664]{1,0:T(4,128)S(1)}, f32[4,1664]{1,0:T(4,128)S(1)}, u32[]{:S(2)}, u32[]{:S(2)}) collective-permute-start(f32[4,1664]{1,0:T(4,128)S(1)} %activate.1.activated), channel_id=1, source_target_pairs={{0,8},{8,0},{1,9},{9,1},{2,10},{10,2},{3,11},{11,3},{4,12},{12,4},... | collective-permute-start | bytes 79880 | tf_op jit(solution)/shard_map/ppermute | solution.py:226

commit v5 on v4

--- a/solution.py
+++ b/solution.py
@@ -153,26 +153,45 @@
     batch = keep.shape[0] // 2
     summed = keep[...] + got[...]
     half = summed.shape[1] - LANES
-    high, low = split(summed[:batch, half:])
-    packed = jnp.concatenate(
-        [summed[:, :half].astype(BF16), jnp.concatenate([high, low], axis=0)], axis=1
+    terms, squares = summed[:, :half], summed[:, half:]
+
+    def exponent(top):
+        return jnp.ceil(jnp.log2(jnp.maximum(top, 1e-30)))
+
+    rows = exponent(jnp.max(jnp.abs(terms), axis=1, keepdims=True))
+    sums = exponent(squares)
+    high, low = split(squares * jnp.exp2(-sums))
+    lane = lax.broadcasted_iota(jnp.int32, squares.shape, 1)
+    extra = jnp.where(
+        lane < LANES // 4,
+        rows,
+        jnp.where(
+            lane < LANES // 2,
+            sums,
+            jnp.where(lane < 3 * LANES // 4, high.astype(F32), low.astype(F32)),
+        ),
     )
+    packed = jnp.concatenate([terms * jnp.exp2(-rows), extra], axis=1)
     middle = packed.shape[1] // 2
-    packed = jnp.concatenate([packed[:, :middle], packed[:, middle:]], axis=0)
-    for piece in range(out.shape[0]):
-        out[piece] = packed
+    out[...] = jnp.concatenate([packed[:, :middle], packed[:, middle:]], axis=0)
 
 
 def activate_kernel(model_width, parts, out):
     batch = out.shape[0]
-    stacked = jnp.sum(parts[...].astype(F32), axis=0)
-    rows = stacked.shape[0] // 2
-    summed = jnp.concatenate([stacked[:rows], stacked[rows:]], axis=1)
     half = out.shape[1]
-    squares = summed[:batch, half : half + 1] + summed[batch:, half : half + 1]
+    terms, squares = 0.0, 0.0
+    for chip in range(parts.shape[0]):
+        rows = parts.shape[1] // 2
+        part = jnp.concatenate([parts[chip, :rows], parts[chip, rows:]], axis=1)
+        extra = part[:, half:]
+        terms = terms + part[:, :half] * jnp.exp2(extra[:, :1])
+        quarter = LANES // 4
+        squares = squares + jnp.exp2(extra[:, quarter : quarter + 1]) * (
+            extra[:, 2 * quarter : 2 * quarter + 1] + extra[:, 3 * quarter : 3 * quarter + 1]
+        )
     scale = lax.rsqrt(squares / model_width + EPSILON)
-    gate = summed[:batch, :half] * scale
-    up = summed[batch:, :half] * scale
+    terms = terms * scale
+    gate, up = terms[:batch], terms[batch:]
     out[...] = (gate / (1.0 + jnp.exp(-gate)) * up).astype(BF16).astype(F32)
 
 
@@ -307,8 +326,9 @@
             gate_keep_kernel, shape(2 * batch, padded), scaled, squares, gate_weight, up_weight
         )
     with jax.named_scope("pair"):
-        hidden = call(pair_kernel, shape(chips, 4 * batch, padded // 2, dtype=BF16), keep, got)
-    hidden = swap(hidden, "chip")
+        hidden = call(pair_kernel, shape(4 * batch, padded // 2), keep, got)
+    hidden = jnp.broadcast_to(hidden.astype(jnp.float16)[None], (chips, *hidden.shape))
+    hidden = swap(hidden, "chip").astype(F32)
     with jax.named_scope("activate"):
         model_width = shards * columns
         activated = call(

time: 74.4 us -> 74.7 us (level)
  no operation moved by 1% of the time
where the time goes in v5:
time: 74.7 us; the launch traced here: 74.4 us
  blocking collectives  64.2 us (86%)
  Pallas kernels  5.38 us (7%)
  starting transfers between devices  3.79 us (5%)
  waiting for transfers between devices  0.85 us (1%)
    all_to_all x5, blocking collectives, swap(): return lax.all_to_all(array, axis, split_axis=0, concat_axis=0, tiled=True)  64.2 us
    pallas_call x10, Pallas kernels, call(): pl.pallas_call(kernel, out_shape=shapes, in_specs=specs or [VMEM] * len(a...  5.38 us
    ppermute x2, starting transfers between devices, other_core(): return lax.ppermute(array, 'core', [(0, 1), (1, 0)])  3.79 us
  transfers between devices with their start and end apart: 2, of which 2 were waited for; matrix products, arithmetic and copies ran while one was open for 0% of the time, Pallas kernels for 1%

profile of v5, /device:TPU:1, one launch (start us, length us, event | category | flops | bytes accessed | tf_op | source)
XLA Modules:
  0.0 74.4 jit_solution(13182251253649995038)
XLA Ops:
  0.0 0.0 copy-start.3
  0.0 0.0 copy-start
  0.0 0.0 copy-start.1
  0.0 0.0 copy-start.2
  0.0 2.0 %attend.1 = (f32[32,4,128]{2,1,0:T(4,128)S(1)}, f32[4,64]{1,0:T(4,128)S(1)}, f32[1,512]{1,0:T(1,128)S(1)}) custom-call(s32[4]{0:T(128)} %refs_0_.1, bf16[4,16,128]{2,1,0:T(8,128)(2,1)} %refs_1_.1, bf16[4,512,128]{2,1,0:T(8,128)(2,1)} %bitcast.5, bf16[4,512,128]{2,1,0:T(8,128)(2,1)} %bitcast.6, f32[4,64]{1,0:T(4,128)} %refs_4_.1, f32[1,512]{1,0:T(1,128)} %bitcast.7, ...), custom_call_target="tpu_custom_call" | custom-call | bytes 2097152 | tf_op jit(solution)/shard_map/attend/pallas_call | solution.py:229
  2.0 16.0 %all_to_all.25.parts = f32[32,4,128]{2,1,0:T(4,128)S(1)} all-to-all(f32[32,4,128]{2,1,0:T(4,128)S(1)} %get-tuple-element.12), channel_id=1, replica_groups=mesh['chip'=16,'core'=2,'kvh'=8] {'chip','core'}, dimensions={0} | all-to-all | bytes 131072 | tf_op jit(solution)/shard_map/all_to_all | solution.py:241
  18.0 0.0 copy-done.3
  18.0 0.6 project.1
  18.5 11.2 %all_to_all.26.parts = bf16[32,16,128]{2,1,0:T(8,128)(2,1)S(1)} all-to-all(bf16[32,16,128]{2,1,0:T(8,128)(2,1)S(1)} %project.1), channel_id=1, replica_groups=mesh['chip'=16,'core'=2,'kvh'=8] {'chip','core'}, dimensions={0} | all-to-all | bytes 262144 | tf_op jit(solution)/shard_map/all_to_all | solution.py:241
  29.7 0.1 carry.1
  29.8 15.2 %all_to_all.27.parts = f32[8,4,512]{2,1,0:T(4,128)S(1)} all-to-all(f32[8,4,512]{2,1,0:T(4,128)S(1)} %carry.1), channel_id=1, replica_groups=mesh['chip'=16,'core'=2,'kvh'=8] {'kvh'}, dimensions={0} | all-to-all | bytes 131072 | tf_op jit(solution)/shard_map/all_to_all | solution.py:241
  45.0 0.0 copy-done
  45.0 0.0 copy-done.1
  45.0 0.0 copy-done.2
  45.0 0.6 gate_up_give.1
  45.6 1.9 %collective-permute-start = (f32[8,1792]{1,0:T(8,128)S(1)}, f32[8,1792]{1,0:T(8,128)S(1)}, u32[]{:S(2)}, u32[]{:S(2)}) collective-permute-start(f32[8,1792]{1,0:T(8,128)S(1)} %get-tuple-element.17), channel_id=1, source_target_pairs={{0,8},{8,0},{1,9},{9,1},{2,10},{10,2},{3,11},{11,3},{4,12},{12,4},... | collective-permute-start | bytes 172040 | tf_op jit(solution)/shard_map/ppermute | solution.py:245
  47.5 0.6 gate_up_keep.1.keep
  48.0 0.3 collective-permute-done.got
  48.4 0.1 pair.1
  48.5 12.9 %all_to_all.28 = f16[16,16,896]{2,1,0:T(8,128)(2,1)S(1)} all-to-all(f16[16,16,896]{2,1,0:T(8,128)(2,1)S(1)} %broadcast_in_dim.2), channel_id=1, replica_groups=mesh['chip'=16,'core'=2,'kvh'=8] {'chip'}, dimensions={0} | all-to-all | bytes 917504 | tf_op jit(solution)/shard_map/all_to_all | solution.py:241
  61.4 0.1 convert_element_type.7.parts
  61.5 0.3 activate.1.activated
  61.7 1.9 %collective-permute-start.1 = (f32[4,1664]{1,0:T(4,128)S(1)}, f32[4,1664]{1,0:T(4,128)S(1)}, u32[]{:S(2)}, u32[]{:S(2)}) collective-permute-start(f32[4,1664]{1,0:T(4,128)S(1)} %activate.1.activated), channel_id=1, source_target_pairs={{0,8},{8,0},{1,9},{9,1},{2,10},{10,2},{3,11},{11,3},{4,12},{12,4},... | collective-permute-start | bytes 79880 | tf_op jit(solution)/shard_map/ppermute | solution.py:245
  63.6 0.3 down_own.1.own
  63.9 0.5 collective-permute-done.1.activated
  64.5 0.4 down.1
  64.9 9.0 %all_to_all.29.parts = f32[8,4,128]{2,1,0:T(4,128)S(1)} all-to-all(f32[8,4,128]{2,1,0:T(4,128)S(1)} %down.1), channel_id=1, replica_groups=mesh['chip'=16,'core'=2,'kvh'=8] {'kvh'}, dimensions={0} | all-to-all | bytes 32768 | tf_op jit(solution)/shard_map/all_to_all | solution.py:241
  73.8 0.6 finish.1
  (2 shorter events, 0.1 us)
Async XLA Ops:
  0.0 18.0 %copy-start.3 = (bf16[1,64,16384]{2,1,0:T(8,128)(2,1)S(1)}, bf16[1,64,16384]{2,1,0:T(8,128)(2,1)}, u32[]{:S(2)}) copy-start(bf16[1,64,16384]{2,1,0:T(8,128)(2,1)} %refs_6_.1) | copy-start | bytes 6291460
  0.0 45.0 %copy-start = (bf16[3328,512]{1,0:T(8,128)(2,1)S(1)}, bf16[3328,512]{1,0:T(8,128)(2,1)}, u32[]{:S(2)}) copy-start(bf16[3328,512]{1,0:T(8,128)(2,1)} %weight.3) | copy-start | bytes 10223620
  0.0 45.0 %copy-start.1 = (bf16[512,3328]{1,0:T(8,128)(2,1)S(1)}, bf16[512,3328]{1,0:T(8,128)(2,1)}, u32[]{:S(2)}) copy-start(bf16[512,3328]{1,0:T(8,128)(2,1)} %gate_weight.3) | copy-start | bytes 10223620
  0.0 45.0 %copy-start.2 = (bf16[512,3328]{1,0:T(8,128)(2,1)S(1)}, bf16[512,3328]{1,0:T(8,128)(2,1)}, u32[]{:S(2)}) copy-start(bf16[512,3328]{1,0:T(8,128)(2,1)} %up_weight.3) | copy-start | bytes 10223620
  45.6 2.8 %collective-permute-start = (f32[8,1792]{1,0:T(8,128)S(1)}, f32[8,1792]{1,0:T(8,128)S(1)}, u32[]{:S(2)}, u32[]{:S(2)}) collective-permute-start(f32[8,1792]{1,0:T(8,128)S(1)} %get-tuple-element.17), channel_id=1, source_target_pairs={{0,8},{8,0},{1,9},{9,1},{2,10},{10,2},{3,11},{11,3},{4,12},{12,4},... | collective-permute-start | bytes 172040 | tf_op jit(solution)/shard_map/ppermute | solution.py:245
  61.7 2.7 %collective-permute-start.1 = (f32[4,1664]{1,0:T(4,128)S(1)}, f32[4,1664]{1,0:T(4,128)S(1)}, u32[]{:S(2)}, u32[]{:S(2)}) collective-permute-start(f32[4,1664]{1,0:T(4,128)S(1)} %activate.1.activated), channel_id=1, source_target_pairs={{0,8},{8,0},{1,9},{9,1},{2,10},{10,2},{3,11},{11,3},{4,12},{12,4},... | collective-permute-start | bytes 79880 | tf_op jit(solution)/shard_map/ppermute | solution.py:245

commit v6 on v4

--- a/solution.py
+++ b/solution.py
@@ -109,8 +109,11 @@
     )
     spread = jnp.concatenate([residual[...]] * (summed.shape[1] // residual.shape[1]), axis=1)
     summed = summed + jnp.where(column_mask(summed.shape, residual.shape[1]), spread, 0.0)
-    for piece in range(out.shape[0]):
-        out[piece] = summed
+    top = jnp.max(jnp.abs(summed), axis=1, keepdims=True)
+    exponent = jnp.ceil(jnp.log2(jnp.maximum(top, 1e-30)))
+    width = summed.shape[1]
+    out[:, :width] = summed * jnp.exp2(-exponent)
+    out[:, width:] = jnp.broadcast_to(exponent, (batch, LANES))
 
 
 def gate_up_half(scaled, core, gate_weight, up_weight):
@@ -127,7 +130,11 @@
     parts, gain, gate_weight, up_weight, _, give, scaled_out, squares_out, carried_out
 ):
     batch = parts.shape[1]
-    carried = jnp.sum(parts[...], axis=0)
+    columns = parts.shape[2] - LANES
+    carried = sum(
+        parts[group, :, :columns] * jnp.exp2(parts[group, :, columns : columns + 1])
+        for group in range(parts.shape[0])
+    )
     width = carried_out.shape[1]
     own = jnp.where(column_mask(carried.shape, width), carried, 0.0)
     carried_out[...] = sum(
@@ -284,8 +291,9 @@
         )
     projected = swap(projected, ("chip", "core"))
     with jax.named_scope("carry"):
-        carried = call(carry_kernel, shape(groups, batch, columns), projected, residual)
-    carried = swap(carried, "kvh")
+        carried = call(carry_kernel, shape(batch, columns + LANES), projected, residual)
+    carried = jnp.broadcast_to(carried.astype(jnp.float16)[None], (groups, *carried.shape))
+    carried = swap(carried, "kvh").astype(F32)
     with jax.named_scope("gate_up_give"):
         give, scaled, squares, own_carried = call(
             gate_give_kernel,

time: 74.4 us -> 74.3 us (level)
  no operation moved by 1% of the time
where the time goes in v6:
time: 74.3 us; the launch traced here: 74.1 us
  blocking collectives  64 us (86%)
  Pallas kernels  5.33 us (7%)
  starting transfers between devices  3.72 us (5%)
  waiting for transfers between devices  0.85 us (1%)
    all_to_all x5, blocking collectives, swap(): return lax.all_to_all(array, axis, split_axis=0, concat_axis=0, tiled=True)  64 us
    pallas_call x10, Pallas kernels, call(): pl.pallas_call(kernel, out_shape=shapes, in_specs=specs or [VMEM] * len(a...  5.33 us
    ppermute x2, starting transfers between devices, other_core(): return lax.ppermute(array, 'core', [(0, 1), (1, 0)])  3.72 us
  transfers between devices with their start and end apart: 2, of which 2 were waited for; matrix products, arithmetic and copies ran while one was open for 0% of the time, Pallas kernels for 1%

profile of v6, /device:TPU:1, one launch (start us, length us, event | category | flops | bytes accessed | tf_op | source)
XLA Modules:
  0.0 74.1 jit_solution(12511990253681053135)
XLA Ops:
  0.0 0.0 copy-start.3
  0.0 0.0 copy-start
  0.0 0.0 copy-start.1
  0.0 0.0 copy-start.2
  0.0 2.0 %attend.1 = (f32[32,4,128]{2,1,0:T(4,128)S(1)}, f32[4,64]{1,0:T(4,128)S(1)}, f32[1,512]{1,0:T(1,128)S(1)}) custom-call(s32[4]{0:T(128)} %refs_0_.1, bf16[4,16,128]{2,1,0:T(8,128)(2,1)} %refs_1_.1, bf16[4,512,128]{2,1,0:T(8,128)(2,1)} %bitcast.5, bf16[4,512,128]{2,1,0:T(8,128)(2,1)} %bitcast.6, f32[4,64]{1,0:T(4,128)} %refs_4_.1, f32[1,512]{1,0:T(1,128)} %bitcast.7, ...), custom_call_target="tpu_custom_call" | custom-call | bytes 2097152 | tf_op jit(solution)/shard_map/attend/pallas_call | solution.py:217
  2.0 16.0 %all_to_all.25.parts = f32[32,4,128]{2,1,0:T(4,128)S(1)} all-to-all(f32[32,4,128]{2,1,0:T(4,128)S(1)} %get-tuple-element.12), channel_id=1, replica_groups=mesh['chip'=16,'core'=2,'kvh'=8] {'chip','core'}, dimensions={0} | all-to-all | bytes 131072 | tf_op jit(solution)/shard_map/all_to_all | solution.py:229
  18.0 0.0 copy-done.3
  18.0 0.6 project.1
  18.5 11.2 %all_to_all.26.parts = bf16[32,16,128]{2,1,0:T(8,128)(2,1)S(1)} all-to-all(bf16[32,16,128]{2,1,0:T(8,128)(2,1)S(1)} %project.1), channel_id=1, replica_groups=mesh['chip'=16,'core'=2,'kvh'=8] {'chip','core'}, dimensions={0} | all-to-all | bytes 262144 | tf_op jit(solution)/shard_map/all_to_all | solution.py:229
  29.7 0.2 carry.1
  29.9 15.0 %all_to_all.27 = f16[8,4,640]{2,1,0:T(4,128)(2,1)S(1)} all-to-all(f16[8,4,640]{2,1,0:T(4,128)(2,1)S(1)} %broadcast_in_dim.2), channel_id=1, replica_groups=mesh['chip'=16,'core'=2,'kvh'=8] {'kvh'}, dimensions={0} | all-to-all | bytes 81920 | tf_op jit(solution)/shard_map/all_to_all | solution.py:229
  45.0 0.0 copy-done
  45.0 0.0 copy-done.1
  45.0 0.0 copy-done.2
  45.0 0.6 gate_up_give.1
  45.6 1.8 %collective-permute-start = (f32[8,1792]{1,0:T(8,128)S(1)}, f32[8,1792]{1,0:T(8,128)S(1)}, u32[]{:S(2)}, u32[]{:S(2)}) collective-permute-start(f32[8,1792]{1,0:T(8,128)S(1)} %get-tuple-element.17), channel_id=1, source_target_pairs={{0,8},{8,0},{1,9},{9,1},{2,10},{10,2},{3,11},{11,3},{4,12},{12,4},... | collective-permute-start | bytes 172040 | tf_op jit(solution)/shard_map/ppermute | solution.py:233
  47.4 0.6 gate_up_keep.1.keep
  48.0 0.3 collective-permute-done.got
  48.4 12.9 %all_to_all.28.parts = bf16[16,16,896]{2,1,0:T(8,128)(2,1)S(1)} all-to-all(bf16[16,16,896]{2,1,0:T(8,128)(2,1)S(1)} %pair.1), channel_id=1, replica_groups=mesh['chip'=16,'core'=2,'kvh'=8] {'chip'}, dimensions={0} | all-to-all | bytes 917504 | tf_op jit(solution)/shard_map/all_to_all | solution.py:229
  61.2 0.1 activate.1.activated
  61.4 1.9 %collective-permute-start.1 = (f32[4,1664]{1,0:T(4,128)S(1)}, f32[4,1664]{1,0:T(4,128)S(1)}, u32[]{:S(2)}, u32[]{:S(2)}) collective-permute-start(f32[4,1664]{1,0:T(4,128)S(1)} %activate.1.activated), channel_id=1, source_target_pairs={{0,8},{8,0},{1,9},{9,1},{2,10},{10,2},{3,11},{11,3},{4,12},{12,4},... | collective-permute-start | bytes 79880 | tf_op jit(solution)/shard_map/ppermute | solution.py:233
  63.3 0.3 down_own.1.own
  63.6 0.5 collective-permute-done.1.activated
  64.1 0.4 down.1
  64.5 9.0 %all_to_all.29.parts = f32[8,4,128]{2,1,0:T(4,128)S(1)} all-to-all(f32[8,4,128]{2,1,0:T(4,128)S(1)} %down.1), channel_id=1, replica_groups=mesh['chip'=16,'core'=2,'kvh'=8] {'kvh'}, dimensions={0} | all-to-all | bytes 32768 | tf_op jit(solution)/shard_map/all_to_all | solution.py:229
  73.5 0.6 finish.1
  (4 shorter events, 0.1 us)
Async XLA Ops:
  0.0 18.0 %copy-start.3 = (bf16[1,64,16384]{2,1,0:T(8,128)(2,1)S(1)}, bf16[1,64,16384]{2,1,0:T(8,128)(2,1)}, u32[]{:S(2)}) copy-start(bf16[1,64,16384]{2,1,0:T(8,128)(2,1)} %refs_6_.1) | copy-start | bytes 6291460
  0.0 45.0 %copy-start = (bf16[3328,512]{1,0:T(8,128)(2,1)S(1)}, bf16[3328,512]{1,0:T(8,128)(2,1)}, u32[]{:S(2)}) copy-start(bf16[3328,512]{1,0:T(8,128)(2,1)} %weight.3) | copy-start | bytes 10223620
  0.0 45.0 %copy-start.1 = (bf16[512,3328]{1,0:T(8,128)(2,1)S(1)}, bf16[512,3328]{1,0:T(8,128)(2,1)}, u32[]{:S(2)}) copy-start(bf16[512,3328]{1,0:T(8,128)(2,1)} %gate_weight.3) | copy-start | bytes 10223620
  0.0 45.0 %copy-start.2 = (bf16[512,3328]{1,0:T(8,128)(2,1)S(1)}, bf16[512,3328]{1,0:T(8,128)(2,1)}, u32[]{:S(2)}) copy-start(bf16[512,3328]{1,0:T(8,128)(2,1)} %up_weight.3) | copy-start | bytes 10223620
  45.6 2.7 %collective-permute-start = (f32[8,1792]{1,0:T(8,128)S(1)}, f32[8,1792]{1,0:T(8,128)S(1)}, u32[]{:S(2)}, u32[]{:S(2)}) collective-permute-start(f32[8,1792]{1,0:T(8,128)S(1)} %get-tuple-element.17), channel_id=1, source_target_pairs={{0,8},{8,0},{1,9},{9,1},{2,10},{10,2},{3,11},{11,3},{4,12},{12,4},... | collective-permute-start | bytes 172040 | tf_op jit(solution)/shard_map/ppermute | solution.py:233
  61.4 2.7 %collective-permute-start.1 = (f32[4,1664]{1,0:T(4,128)S(1)}, f32[4,1664]{1,0:T(4,128)S(1)}, u32[]{:S(2)}, u32[]{:S(2)}) collective-permute-start(f32[4,1664]{1,0:T(4,128)S(1)} %activate.1.activated), channel_id=1, source_target_pairs={{0,8},{8,0},{1,9},{9,1},{2,10},{10,2},{3,11},{11,3},{4,12},{12,4},... | collective-permute-start | bytes 79880 | tf_op jit(solution)/shard_map/ppermute | solution.py:233

commit v7 on v4

--- a/solution.py
+++ b/solution.py
@@ -123,30 +123,35 @@
     return jnp.concatenate([gate[:batch] + gate[batch:], up[:batch] + up[batch:]], axis=0)
 
 
-def gate_give_kernel(
-    parts, gain, gate_weight, up_weight, _, give, scaled_out, squares_out, carried_out
-):
-    batch = parts.shape[1]
+def square_sums(carried):
+    sums = jnp.sum(carried * carried, axis=1, keepdims=True)
+    return jnp.broadcast_to(
+        jnp.concatenate([sums, sums], axis=0), (2 * carried.shape[0], LANES)
+    )
+
+
+def gate_give_kernel(parts, gain, gate_weight, up_weight, _, give, carried_out):
     carried = jnp.sum(parts[...], axis=0)
-    width = carried_out.shape[1]
+    carried_out[...] = carried
+    half = gate_weight.shape[1] // CORES
+    give[:, :half] = gate_up_half(
+        carried * gain[...], 1 - lax.axis_index("core"), gate_weight, up_weight
+    )
+    give[:, half:] = square_sums(carried)
+
+
+def gate_keep_kernel(carried_in, gain, gate_weight, up_weight, keep, own_out):
+    carried = carried_in[...]
+    half = gate_weight.shape[1] // CORES
+    keep[:, :half] = gate_up_half(
+        carried * gain[...], lax.axis_index("core"), gate_weight, up_weight
+    )
+    keep[:, half:] = square_sums(carried)
+    width = own_out.shape[1]
     own = jnp.where(column_mask(carried.shape, width), carried, 0.0)
-    carried_out[...] = sum(
+    own_out[...] = sum(
         own[:, piece * width : (piece + 1) * width] for piece in range(carried.shape[1] // width)
     )
-    squares = jnp.sum(carried * carried, axis=1, keepdims=True)
-    squares = jnp.broadcast_to(jnp.concatenate([squares, squares], axis=0), (2 * batch, LANES))
-    scaled = carried * gain[...]
-    half = gate_weight.shape[1] // CORES
-    give[:, :half] = gate_up_half(scaled, 1 - lax.axis_index("core"), gate_weight, up_weight)
-    give[:, half:] = squares
-    scaled_out[...] = scaled
-    squares_out[...] = squares
-
-
-def gate_keep_kernel(scaled, squares, gate_weight, up_weight, keep):
-    half = gate_weight.shape[1] // CORES
-    keep[:, :half] = gate_up_half(scaled[...], lax.axis_index("core"), gate_weight, up_weight)
-    keep[:, half:] = squares[...]
 
 
 def pair_kernel(keep, got, out):
@@ -287,14 +292,9 @@
         carried = call(carry_kernel, shape(groups, batch, columns), projected, residual)
     carried = swap(carried, "kvh")
     with jax.named_scope("gate_up_give"):
-        give, scaled, squares, own_carried = call(
+        give, carried = call(
             gate_give_kernel,
-            (
-                shape(2 * batch, padded),
-                shape(batch, columns),
-                shape(2 * batch, LANES),
-                shape(batch, own),
-            ),
+            (shape(2 * batch, padded), shape(batch, columns)),
             carried,
             gain,
             gate_weight,
@@ -303,8 +303,13 @@
         )
     got = other_core(give)
     with jax.named_scope("gate_up_keep"):
-        keep = call(
-            gate_keep_kernel, shape(2 * batch, padded), scaled, squares, gate_weight, up_weight
+        keep, own_carried = call(
+            gate_keep_kernel,
+            (shape(2 * batch, padded), shape(batch, own)),
+            carried,
+            gain,
+            gate_weight,
+            up_weight,
         )
     with jax.named_scope("pair"):
         hidden = call(pair_kernel, shape(chips, 4 * batch, padded // 2, dtype=BF16), keep, got)

time: 74.4 us -> 74.4 us (level)
  no operation moved by 1% of the time
where the time goes in v7:
time: 74.4 us; the launch traced here: 74.1 us
  blocking collectives  64.2 us (86%)
  Pallas kernels  5.2 us (7%)
  starting transfers between devices  3.79 us (5%)
  waiting for transfers between devices  0.85 us (1%)
    all_to_all x5, blocking collectives, swap(): return lax.all_to_all(array, axis, split_axis=0, concat_axis=0, tiled=True)  64.2 us
    pallas_call x10, Pallas kernels, call(): pl.pallas_call(kernel, out_shape=shapes, in_specs=specs or [VMEM] * len(a...  5.2 us
    ppermute x2, starting transfers between devices, other_core(): return lax.ppermute(array, 'core', [(0, 1), (1, 0)])  3.79 us
  transfers between devices with their start and end apart: 2, of which 2 were waited for; matrix products, arithmetic and copies ran while one was open for 0% of the time, Pallas kernels for 1%

profile of v7, /device:TPU:1, one launch (start us, length us, event | category | flops | bytes accessed | tf_op | source)
XLA Modules:
  0.0 74.1 jit_solution(12077958270616951361)
XLA Ops:
  0.0 0.0 copy-start.3
  0.0 0.0 copy-start
  0.0 0.0 copy-start.1
  0.0 0.0 copy-start.2
  0.0 2.0 %attend.1 = (f32[32,4,128]{2,1,0:T(4,128)S(1)}, f32[4,64]{1,0:T(4,128)S(1)}, f32[1,512]{1,0:T(1,128)S(1)}) custom-call(s32[4]{0:T(128)} %refs_0_.1, bf16[4,16,128]{2,1,0:T(8,128)(2,1)} %refs_1_.1, bf16[4,512,128]{2,1,0:T(8,128)(2,1)} %bitcast.5, bf16[4,512,128]{2,1,0:T(8,128)(2,1)} %bitcast.6, f32[4,64]{1,0:T(4,128)} %refs_4_.1, f32[1,512]{1,0:T(1,128)} %bitcast.7, ...), custom_call_target="tpu_custom_call" | custom-call | bytes 2097152 | tf_op jit(solution)/shard_map/attend/pallas_call | solution.py:215
  2.0 16.0 %all_to_all.25.parts = f32[32,4,128]{2,1,0:T(4,128)S(1)} all-to-all(f32[32,4,128]{2,1,0:T(4,128)S(1)} %get-tuple-element.12), channel_id=1, replica_groups=mesh['chip'=16,'core'=2,'kvh'=8] {'chip','core'}, dimensions={0} | all-to-all | bytes 131072 | tf_op jit(solution)/shard_map/all_to_all | solution.py:227
  18.0 0.0 copy-done.3
  18.0 0.6 project.1
  18.5 11.2 %all_to_all.26.parts = bf16[32,16,128]{2,1,0:T(8,128)(2,1)S(1)} all-to-all(bf16[32,16,128]{2,1,0:T(8,128)(2,1)S(1)} %project.1), channel_id=1, replica_groups=mesh['chip'=16,'core'=2,'kvh'=8] {'chip','core'}, dimensions={0} | all-to-all | bytes 262144 | tf_op jit(solution)/shard_map/all_to_all | solution.py:227
  29.7 0.1 carry.1
  29.8 15.2 %all_to_all.27.parts = f32[8,4,512]{2,1,0:T(4,128)S(1)} all-to-all(f32[8,4,512]{2,1,0:T(4,128)S(1)} %carry.1), channel_id=1, replica_groups=mesh['chip'=16,'core'=2,'kvh'=8] {'kvh'}, dimensions={0} | all-to-all | bytes 131072 | tf_op jit(solution)/shard_map/all_to_all | solution.py:227
  45.0 0.0 copy-done
  45.0 0.0 copy-done.1
  45.0 0.0 copy-done.2
  45.0 0.6 gate_up_give.1
  45.6 1.9 %collective-permute-start = (f32[8,1792]{1,0:T(8,128)S(1)}, f32[8,1792]{1,0:T(8,128)S(1)}, u32[]{:S(2)}, u32[]{:S(2)}) collective-permute-start(f32[8,1792]{1,0:T(8,128)S(1)} %get-tuple-element.17), channel_id=1, source_target_pairs={{0,8},{8,0},{1,9},{9,1},{2,10},{10,2},{3,11},{11,3},{4,12},{12,4},... | collective-permute-start | bytes 172040 | tf_op jit(solution)/shard_map/ppermute | solution.py:231
  47.5 0.6 gate_up_keep.1
  48.1 0.3 collective-permute-done.got
  48.4 12.9 %all_to_all.28.parts = bf16[16,16,896]{2,1,0:T(8,128)(2,1)S(1)} all-to-all(bf16[16,16,896]{2,1,0:T(8,128)(2,1)S(1)} %pair.1), channel_id=1, replica_groups=mesh['chip'=16,'core'=2,'kvh'=8] {'chip'}, dimensions={0} | all-to-all | bytes 917504 | tf_op jit(solution)/shard_map/all_to_all | solution.py:227
  61.3 0.1 activate.1.activated
  61.4 1.9 %collective-permute-start.1 = (f32[4,1664]{1,0:T(4,128)S(1)}, f32[4,1664]{1,0:T(4,128)S(1)}, u32[]{:S(2)}, u32[]{:S(2)}) collective-permute-start(f32[4,1664]{1,0:T(4,128)S(1)} %activate.1.activated), channel_id=1, source_target_pairs={{0,8},{8,0},{1,9},{9,1},{2,10},{10,2},{3,11},{11,3},{4,12},{12,4},... | collective-permute-start | bytes 79880 | tf_op jit(solution)/shard_map/ppermute | solution.py:231
  63.3 0.3 down_own.1.own
  63.6 0.5 collective-permute-done.1.activated
  64.1 0.4 down.1
  64.5 9.0 %all_to_all.29.parts = f32[8,4,128]{2,1,0:T(4,128)S(1)} all-to-all(f32[8,4,128]{2,1,0:T(4,128)S(1)} %down.1), channel_id=1, replica_groups=mesh['chip'=16,'core'=2,'kvh'=8] {'kvh'}, dimensions={0} | all-to-all | bytes 32768 | tf_op jit(solution)/shard_map/all_to_all | solution.py:227
  73.5 0.6 finish.1
  (1 shorter events, 0.0 us)
Async XLA Ops:
  0.0 18.0 %copy-start.3 = (bf16[1,64,16384]{2,1,0:T(8,128)(2,1)S(1)}, bf16[1,64,16384]{2,1,0:T(8,128)(2,1)}, u32[]{:S(2)}) copy-start(bf16[1,64,16384]{2,1,0:T(8,128)(2,1)} %refs_6_.1) | copy-start | bytes 6291460
  0.0 45.0 %copy-start = (bf16[3328,512]{1,0:T(8,128)(2,1)S(1)}, bf16[3328,512]{1,0:T(8,128)(2,1)}, u32[]{:S(2)}) copy-start(bf16[3328,512]{1,0:T(8,128)(2,1)} %weight.3) | copy-start | bytes 10223620
  0.0 45.0 %copy-start.1 = (bf16[512,3328]{1,0:T(8,128)(2,1)S(1)}, bf16[512,3328]{1,0:T(8,128)(2,1)}, u32[]{:S(2)}) copy-start(bf16[512,3328]{1,0:T(8,128)(2,1)} %gate_weight.3) | copy-start | bytes 10223620
  0.0 45.0 %copy-start.2 = (bf16[512,3328]{1,0:T(8,128)(2,1)S(1)}, bf16[512,3328]{1,0:T(8,128)(2,1)}, u32[]{:S(2)}) copy-start(bf16[512,3328]{1,0:T(8,128)(2,1)} %up_weight.3) | copy-start | bytes 10223620
  45.6 2.8 %collective-permute-start = (f32[8,1792]{1,0:T(8,128)S(1)}, f32[8,1792]{1,0:T(8,128)S(1)}, u32[]{:S(2)}, u32[]{:S(2)}) collective-permute-start(f32[8,1792]{1,0:T(8,128)S(1)} %get-tuple-element.17), channel_id=1, source_target_pairs={{0,8},{8,0},{1,9},{9,1},{2,10},{10,2},{3,11},{11,3},{4,12},{12,4},... | collective-permute-start | bytes 172040 | tf_op jit(solution)/shard_map/ppermute | solution.py:231
  61.4 2.7 %collective-permute-start.1 = (f32[4,1664]{1,0:T(4,128)S(1)}, f32[4,1664]{1,0:T(4,128)S(1)}, u32[]{:S(2)}, u32[]{:S(2)}) collective-permute-start(f32[4,1664]{1,0:T(4,128)S(1)} %activate.1.activated), channel_id=1, source_target_pairs={{0,8},{8,0},{1,9},{9,1},{2,10},{10,2},{3,11},{11,3},{4,12},{12,4},... | collective-permute-start | bytes 79880 | tf_op jit(solution)/shard_map/ppermute | solution.py:231
